TPU v7x, 256 devices: a whole 4x4x8 slice. The times are simulated.
256 devices in a mesh: replica: 16 (over y_lo, z), shard: 16 (over y_hi, x, core).
Axes of the slice: x: 4, y: 4 (y_hi: 2, y_lo: 2; y = y_hi * 2 + y_lo), z: 8, core: 2. Of those that a mesh axis runs over, the one named last changes fastest.
Arguments:
- grad_key: bfloat16 [16, 1024, 8192], P('replica', 'shard')
- error_key: bfloat16 [16, 1024, 8192], P('replica', 'shard'), may hold values from -3 to 3
- prev_key: bfloat16 [8192, 64], P('shard'), may hold values from -6 to 6
- grad_val: bfloat16 [16, 1024, 8192], P('replica', 'shard')
- error_val: bfloat16 [16, 1024, 8192], P('replica', 'shard'), may hold values from -3 to 3
- prev_val: bfloat16 [8192, 64], P('shard'), may hold values from -6 to 6
Outputs:
- update_key: bfloat16 [1024, 8192], P('shard')
- next_error_key: bfloat16 [16, 1024, 8192], P('replica', 'shard')
- factor_key: float32 [8192, 64], P('shard')
- update_val: bfloat16 [1024, 8192], P('shard')
- next_error_val: bfloat16 [16, 1024, 8192], P('replica', 'shard')
- factor_val: float32 [8192, 64], P('shard')
All inputs are finite; a program needn't handle non-finite values.
Results may differ from a plain program's by a relative error of at most 0.012.
Values may be sent and summed in bfloat16 or wider, within the bound.
A program may use at most 64 MiB of HBM per device.

v0:
```python
import jax
import jax.numpy as jnp
from jax import lax
from jax.sharding import PartitionSpec as P


def merge_local(grads, errors):
    return (grads[0].astype(jnp.float32) + errors[0].astype(jnp.float32)).astype(jnp.bfloat16)


def gram_of(left):
    return jnp.dot(left.T, left, precision=lax.Precision.HIGHEST)


def orthonormal(left, gram):
    rank_size = left.shape[1]
    ridged = gram + 1e-06 * (jnp.trace(gram) / rank_size) * jnp.eye(rank_size, dtype=jnp.float32)
    lower = jnp.linalg.cholesky(ridged)
    return lax.linalg.triangular_solve(lower, left, left_side=False, lower=True, transpose_a=True)


def project(merged, previous, replicas):
    gathered = lax.all_gather(previous, "shard", axis=0, tiled=True)
    partial_value = jnp.dot(merged, gathered, preferred_element_type=jnp.float32)
    left = lax.psum(partial_value, "replica") / replicas
    gram = lax.psum(gram_of(left), "shard")
    return orthonormal(left, gram)


def expand(merged, ortho, replicas):
    ortho_b = ortho.astype(jnp.bfloat16)
    col_count = merged.shape[1]
    pieces = lax.axis_size("shard")
    slice_len = col_count // pieces
    q_term = jnp.einsum("nc,nk->ck", merged, ortho_b, preferred_element_type=jnp.float32)
    q_whole = lax.psum(q_term, ("replica", "shard")) / replicas
    factor = lax.dynamic_slice_in_dim(q_whole, lax.axis_index("shard") * slice_len, slice_len, 0)
    factor_b = q_whole.astype(jnp.bfloat16)
    approx = jnp.einsum("nk,ck->nc", ortho_b, factor_b, preferred_element_type=jnp.float32)
    update = approx.astype(jnp.bfloat16)
    next_error = (merged.astype(jnp.float32) - approx).astype(jnp.bfloat16)[None]
    return (update, next_error, factor)


def per_device(grad_key, error_key, prev_key, grad_val, error_val, prev_val):
    replicas = lax.axis_size("replica")
    merged_key = merge_local(grad_key, error_key)
    merged_val = merge_local(grad_val, error_val)
    ortho_key = project(merged_key, prev_key, replicas)
    ortho_val = project(merged_val, prev_val, replicas)
    update_key, next_error_key, factor_key = expand(merged_key, ortho_key, replicas)
    update_val, next_error_val, factor_val = expand(merged_val, ortho_val, replicas)
    return (update_key, next_error_key, factor_key, update_val, next_error_val, factor_val)


def solution(mesh):
    in_specs = (
        P("replica", "shard", None),
        P("replica", "shard", None),
        P("shard", None),
        P("replica", "shard", None),
        P("replica", "shard", None),
        P("shard", None),
    )
    out_specs = (
        P("shard", None),
        P("replica", "shard", None),
        P("shard", None),
        P("shard", None),
        P("replica", "shard", None),
        P("shard", None),
    )
    return jax.shard_map(
        per_device, mesh=mesh, in_specs=in_specs, out_specs=out_specs, check_vma=False
    )
```

profile of v0, /device:TPU:1, one launch (start us, length us, event | category | flops | bytes accessed | tf_op | source)
XLA Modules:
  0.0 556.3 jit_solution(3946683418601852659)
XLA Ops:
  7.2 0.0 copy-start.2
  7.2 0.0 all-gather.5.cloned.1.call-start
  7.2 0.7 all-gather.5.cloned.1.call-update
  7.9 0.0 all-gather.3.cloned.1.call-start
  8.0 0.7 all-gather.3.cloned.1.call-update
  8.7 0.0 all-reduce.5.cloned.1.call-start
  8.7 56.6 %all-gather.5.cloned.1.call-done = bf16[8192,64]{0,1:T(8,128)(2,1)} async-done(((bf16[512,64]{0,1:T(8,128)(2,1)}), bf16[8192,64]{0,1:T(8,128)(2,1)}) %all-gather.5.cloned.1.call-update) | async-done | bytes 1048592 | tf_op jit(solution)/shard_map/all_gather | solution.py:23
  65.3 2.3 fusion.32
  67.6 0.0 copy-start
  67.6 0.0 copy-start.1
  67.6 49.6 %all-gather.3.cloned.1.call-done = bf16[8192,64]{0,1:T(8,128)(2,1)} async-done(((bf16[512,64]{0,1:T(8,128)(2,1)}), bf16[8192,64]{0,1:T(8,128)(2,1)}) %all-gather.3.cloned.1.call-update) | async-done | bytes 1048592 | tf_op jit(solution)/shard_map/all_gather | solution.py:23
  117.2 0.0 copy-done.2
  117.2 2.0 fusion.36
  119.1 49.1 %all-reduce.2 = (f32[64,64]{1,0:T(8,128)S(1)}, f32[64,64]{1,0:T(8,128)S(1)}) all-reduce(f32[64,64]{1,0:T(8,128)S(1)} %fusion.36, f32[64,64]{1,0:T(8,128)S(1)} %fusion.32), channel_id=1, replica_groups=mesh['replica'=16,'shard'=16] {'replica'}, use_global_device_ids=true, to_apply=%region_0.0 | all-reduce | flops 8192 | bytes 65536 | tf_op jit(solution)/shard_map/psum | solution.py:25
  168.2 0.2 fusion.17
  168.5 0.2 fusion.20
  168.7 73.4 %all-reduce.1 = (f32[64,64]{0,1:T(8,128)S(1)}, f32[64,64]{0,1:T(8,128)S(1)}) all-reduce(f32[64,64]{0,1:T(8,128)S(1)} %fusion.20, f32[64,64]{0,1:T(8,128)S(1)} %fusion.17), channel_id=1, replica_groups=mesh['replica'=16,'shard'=16] {'shard'}, use_global_device_ids=true, to_apply=%region_1.0 | all-reduce | flops 8192 | bytes 65536 | tf_op jit(solution)/shard_map/psum | solution.py:26
  242.1 0.6 select_reduce_fusion.3
  242.7 0.6 select_reduce_fusion.2
  244.6 0.1 copy.15
  244.7 5.8 %cholesky.55 = f32[64,64]{1,0:T(8,128)S(1)} custom-call(f32[64,64]{1,0:T(8,128)S(1)} %fusion.13), custom_call_target="Cholesky" | custom-call | tf_op jit(solution)/shard_map/jit(cholesky)/cholesky | solution.py:18
  250.6 0.6 compare_reduce_fusion
  251.2 0.7 fusion.11
  251.9 4.9 custom-call.7
  256.8 0.3 fusion.1
  257.0 0.0 copy-done
  257.1 0.0 copy-done.1
  257.1 1.8 fusion.30
  258.8 0.1 copy.13
  258.9 5.8 %cholesky.44 = f32[64,64]{1,0:T(8,128)S(1)} custom-call(f32[64,64]{1,0:T(8,128)S(1)} %fusion.15), custom_call_target="Cholesky" | custom-call | tf_op jit(solution)/shard_map/jit(cholesky)/cholesky | solution.py:18
  264.8 0.6 compare_reduce_fusion.1
  265.5 0.7 fusion.10
  266.1 4.9 custom-call.6
  271.0 0.3 fusion
  271.3 3.0 fusion.34
  274.3 0.0 all-reduce.5.cloned.1.call-update
  274.3 265.8 %all-reduce.5.cloned.1.call-done = (f32[8192,64]{0,1:T(8,128)}, f32[8192,64]{0,1:T(8,128)}) async-done(((f32[8192,64]{0,1:T(8,128)}, f32[8192,64]{0,1:T(8,128)}), (f32[8192,64]{0,1:T(8,128)}, f32[8192,64]{0,1:T(8,128)})) %all-reduce.5.cloned.1.call-update) | async-done | bytes 4194320 | tf_op jit(solution)/shard_map/psum | solution.py:36
  540.1 0.0 copy-start.5
  540.1 3.6 fusion.5
  543.7 0.0 copy-done.5
  543.7 0.0 copy-start.4
  543.7 0.2 broadcast_multiply_fusion
  543.9 1.4 copy-done.4
  545.3 0.0 copy-start.3
  545.3 0.2 broadcast_multiply_fusion.1
  545.5 1.1 copy-done.3
  546.5 1.9 fusion.3
  548.4 0.7 constant_dynamic-slice_fusion
  549.1 0.7 constant_dynamic-slice_fusion.1
  (5 shorter events, 0.1 us)
Async XLA Ops:
  7.2 110.0 %copy-start.2 = (bf16[1,64,8192]{2,1,0:T(8,128)(2,1)S(1)}, bf16[1,64,8192]{2,1,0:T(8,128)(2,1)}, u32[]{:S(2)}) copy-start(bf16[1,64,8192]{2,1,0:T(8,128)(2,1)} %param.10) | copy-start | bytes 3145732
  7.2 58.1 %all-gather.5.cloned.1.call-start = ((), (), s32[]{:S(2)}) async-start(), calls=%async_computation.1 | async-start | bytes 1114112 | tf_op jit(solution)/shard_map/all_gather | solution.py:23
  7.9 109.2 %all-gather.3.cloned.1.call-start = ((), (), s32[]{:S(2)}) async-start(), calls=%async_computation | async-start | bytes 1114112 | tf_op jit(solution)/shard_map/all_gather | solution.py:23
  8.7 531.5 %all-reduce.5.cloned.1.call-start = ((), (), s32[]{:S(2)}) async-start(), calls=%async_computation.2 | async-start | bytes 8388608 | tf_op jit(solution)/shard_map/psum | solution.py:36
  67.6 189.5 %copy-start = (bf16[1,64,8192]{2,1,0:T(8,128)(2,1)S(1)}, bf16[1,64,8192]{2,1,0:T(8,128)(2,1)}, u32[]{:S(2)}) copy-start(bf16[1,64,8192]{2,1,0:T(8,128)(2,1)} %param.13) | copy-start | bytes 3145732
  67.6 189.5 %copy-start.1 = (bf16[1,64,8192]{2,1,0:T(8,128)(2,1)S(1)}, bf16[1,64,8192]{2,1,0:T(8,128)(2,1)}, u32[]{:S(2)}) copy-start(bf16[1,64,8192]{2,1,0:T(8,128)(2,1)} %param.12) | copy-start | bytes 3145732
  540.1 3.6 copy-start.5
  543.7 1.6 copy-start.4
  545.3 1.2 copy-start.3
Sparse Core Ops, SparseCore 0:
  10.6 54.6 all-gather.4
  67.8 49.2 all-gather.2
  274.4 265.6 all-reduce.4
where the time goes:
time: 557 us; the launch traced here: 556 us
  waiting for transfers between devices  373 us (67%)
  blocking collectives  122 us (22%)
  other arithmetic  25.7 us (5%)
  matrix products  15.5 us (3%)
  between operations  15.2 us (3%)
    psum x1, waiting for transfers between devices, expand(): q_whole = lax.psum(q_term, ('replica', 'shard')) / replicas  266 us
    all_gather x2, waiting for transfers between devices, project(): gathered = lax.all_gather(previous, 'shard', axis=0, tiled=True)  106 us
    psum x1, blocking collectives, project(): gram = lax.psum(gram_of(left), 'shard')  73.4 us
    psum x1, blocking collectives, project(): left = lax.psum(partial_value, 'replica') / replicas  49.1 us
    another operation x6, other arithmetic, orthonormal(): lower = jnp.linalg.cholesky(ridged)  13 us
  transfers between devices with their start and end apart: 3, of which 3 were waited for; matrix products, arithmetic and copies ran while one was open for 0% of the time, Pallas kernels for 0%

commit v1 on v0

v1 whole, which is shorter than its diff:
```python
import functools

import jax
import jax.numpy as jnp
from jax import lax
from jax.experimental import pallas as pl
from jax.experimental.pallas import tpu as pltpu
from jax.sharding import PartitionSpec as P

MESH = pl.DeviceIdType.MESH
F32, BF16 = jnp.float32, jnp.bfloat16
NX, NY, NZ, NC = 4, 4, 8, 2
REPLICAS = 16
RANK = 64
ROWS = 64
BLK = 512
BLKS = 16
RIDGE = 1e-6
NT = (((1,), (1,)), ((), ()))
NN = (((1,), (0,)), ((), ()))


def device(x, y, z, c):
    return (lax.rem(y, 2) * NZ + z, (lax.div(y, 2) * NX + x) * NC + c)


def send(src, dst, ssem, rsem, dev):
    copy = pltpu.make_async_remote_copy(
        src_ref=src, dst_ref=dst, send_sem=ssem, recv_sem=rsem, device_id=dev, device_id_type=MESH
    )
    copy.start()
    return copy


def arrival(dst, ssem, rsem, dev):
    pltpu.make_async_remote_copy(
        src_ref=dst, dst_ref=dst, send_sem=ssem, recv_sem=rsem, device_id=dev, device_id_type=MESH
    ).wait_recv()


def lanes_low(shape):
    return lax.broadcasted_iota(jnp.int32, shape, 1) < RANK


def solve_rows(gram, left):
    shape = (RANK, 128)
    row = lax.broadcasted_iota(jnp.int32, shape, 0)
    lane = lax.broadcasted_iota(jnp.int32, shape, 1)
    low = lane < RANK
    swapped = pltpu.roll(left, RANK, 1)
    out = []
    for side in range(2):
        here = low if side == 0 else jnp.logical_not(low)
        diag = lane == row + side * RANK
        trace = jnp.sum(jnp.where(diag, gram, 0.0))
        ridge = RIDGE * (trace / RANK)
        whole = jnp.where(here, gram + jnp.where(diag, ridge, 0.0), swapped)
        out.append([whole[8 * t : 8 * t + 8] for t in range(8)])
    sub = lax.broadcasted_iota(jnp.int32, (8, 128), 0)
    for j in range(RANK - 1):
        top, pos = divmod(j, 8)
        for side in range(2):
            tiles = out[side]
            col = side * RANK + j
            pivot_row = tiles[top][pos : pos + 1, :]
            inv = 1.0 / pivot_row[:, col : col + 1]
            scaled = pivot_row * inv
            for t in range(top, 8):
                if t == top:
                    if pos == 7:
                        continue
                    factor = jnp.where(sub > pos, jnp.broadcast_to(tiles[t][:, col : col + 1], (8, 128)), 0.0)
                else:
                    factor = tiles[t][:, col : col + 1]
                tiles[t] = tiles[t] - factor * scaled
    done = []
    for side in range(2):
        whole = jnp.concatenate(out[side], axis=0)
        diag = lane == row + side * RANK
        pivots = jnp.sum(jnp.where(diag, whole, 0.0), axis=1, keepdims=True)
        done.append(pltpu.roll(whole * lax.rsqrt(pivots), RANK, 1))
    return jnp.where(low, done[0], 0.0), jnp.where(low, 0.0, done[1])


def step_kernel(
    gk, ek, pk, gv, ev, pv,
    m_out, o_out, f_out,
    grads, errors, mbuf, pbuf, acc, lbuf, r1, lt2, gp, cpair, c1, cfull, obl,
    obuf, wbuf, pr, s1, r2, s2, r3, s3, r4, fbuf,
    load_sem, out_sem,
    a_ss, a_rs, af_ss, af_rs, b_ss, b_rs, b2_ss, b2_rs, c0_ss, c0_rs, c1_ss, c1_rs, c2_ss, c2_rs,
    e0_ss, e0_rs, e1_ss, e1_rs, e2_ss, e2_rs, e3_ss, e3_rs,
    g3_ss, g3_rs, g2_ss, g2_rs, g1_ss, g1_rs, g0_ss, g0_rs,
):
    r = lax.axis_index("replica")
    s = lax.axis_index("shard")
    y_lo, z = lax.div(r, NZ), lax.rem(r, NZ)
    y_hi, x, c = lax.div(s, NX * NC), lax.rem(lax.div(s, NC), NX), lax.rem(s, NC)
    y = 2 * y_hi + y_lo
    oc = 1 - c
    cross = lax.rem(y + 3 + 2 * y_lo, NY)
    flip = 2 * y_hi + 1 - y_lo
    mate = device(x, y, z, oc)

    def at_x(d):
        return lax.rem(x + d, NX)

    def at_y(d):
        return lax.rem(y + d, NY)

    def at_z(d):
        return lax.rem(z + d, NZ)

    loads = [
        pltpu.make_async_copy(gk.at[0], grads.at[0], load_sem.at[0]),
        pltpu.make_async_copy(ek.at[0], errors.at[0], load_sem.at[1]),
        pltpu.make_async_copy(gv.at[0], grads.at[1], load_sem.at[2]),
        pltpu.make_async_copy(ev.at[0], errors.at[1], load_sem.at[3]),
    ]
    own_prev = [
        pltpu.make_async_copy(pk, pbuf.at[s, pl.ds(0, RANK)], load_sem.at[4]),
        pltpu.make_async_copy(pv, pbuf.at[s, pl.ds(RANK, RANK)], load_sem.at[5]),
    ]
    for copy in own_prev + loads:
        copy.start()

    partners = [device(x, flip, at_z(d), c) for d in (4, 3, 5, 2, 6, 1, 7)]
    partners += [device(x, y, at_z(d), c) for d in (4, 3, 5, 2, 6, 1, 7)]
    partners += [device(at_x(d), cross, z, c) for d in (2, 1, 3)]
    partners += [device(at_x(d), y, z, c) for d in (2, 1, 3)]
    partners += [device(x, at_y(d), z, c) for d in (2, 1, 3)]
    partners += [mate]
    barrier = pltpu.get_barrier_semaphore()
    for dev in partners:
        pl.semaphore_signal(barrier, inc=1, device_id=dev, device_id_type=MESH)
    for copy in own_prev:
        copy.wait()
    pl.semaphore_wait(barrier, len(partners))

    sent = []

    far = [(2, 1), (1, 1), (3, 1), (2, 0), (1, 0), (3, 0), (0, 1)]
    for i, (dx, over) in enumerate(far):
        dev = device(at_x(dx), cross if over else y, z, c)
        sent.append(send(pbuf.at[s], pbuf.at[s], a_ss.at[i], a_rs.at[i], dev))
    sent.append(send(pbuf.at[s], pbuf.at[s], af_ss.at[7], af_rs.at[7], mate))

    for copy in loads:
        copy.wait()

    def merge(b, carry):
        cols = pl.ds(pl.multiple_of(b * BLK, BLK), BLK)
        for m in range(2):
            total = grads[m, :, cols].astype(F32) + errors[m, :, cols].astype(F32)
            mbuf[b, m * ROWS : (m + 1) * ROWS, :] = total.astype(BF16)
        return carry

    lax.fori_loop(0, BLKS, merge, 0)
    store_m = pltpu.make_async_copy(mbuf, m_out, out_sem.at[0])
    store_m.start()

    def left_term(slot):
        return lax.dot_general(pbuf[slot], mbuf[slot], NT, preferred_element_type=F32)

    acc[...] = left_term(s)
    order = (6, 4, 5, 3, 1, 2, 0)
    slots = []
    for i, (dx, over) in enumerate(far):
        yy = (1 - y_hi) if over else y_hi
        slots.append((yy * NX + lax.rem(x + NX - dx, NX)) * NC)
    for i in order:
        slot = slots[i] + c
        arrival(pbuf.at[slot], a_ss.at[i], a_rs.at[i], mate)
        sent.append(send(pbuf.at[slot], pbuf.at[slot], af_ss.at[i], af_rs.at[i], mate))
        acc[...] += left_term(slot)
    for i in (7,) + order:
        slot = (s + oc - c) if i == 7 else slots[i] + oc
        arrival(pbuf.at[slot], af_ss.at[i], af_rs.at[i], mate)
        acc[...] += left_term(slot)

    low64 = lanes_low((RANK, 128))
    part = jnp.where(low64, acc[0:RANK, :], acc[RANK:, :])
    for t in range(NZ):
        lbuf[t] = part[8 * t : 8 * t + 8]
    r1[r] = lbuf[z]
    peers = [(1, d) for d in (4, 3, 5, 2, 6, 1, 7, 0)] + [(0, d) for d in (4, 3, 5, 2, 6, 1, 7)]
    for i, (over, dz) in enumerate(peers):
        dev = device(x, flip if over else y, at_z(dz), c)
        sent.append(send(lbuf.at[at_z(dz)], r1.at[r], b_ss.at[i], b_rs.at[i], dev))
    for i, (over, dz) in enumerate(peers):
        slot = ((1 - y_lo) if over else y_lo) * NZ + lax.rem(z + NZ - dz, NZ)
        arrival(r1.at[slot], b_ss.at[i], b_rs.at[i], mate)
    total = r1[0]
    for t in range(1, REPLICAS):
        total = total + r1[t]
    lt2[z] = total / REPLICAS
    zs = (4, 3, 5, 2, 6, 1, 7)
    for i, dz in enumerate(zs):
        sent.append(send(lt2.at[z], lt2.at[z], b2_ss.at[i], b2_rs.at[i], device(x, y, at_z(dz), c)))
    for i, dz in enumerate(zs):
        arrival(lt2.at[lax.rem(z + NZ - dz, NZ)], b2_ss.at[i], b2_rs.at[i], mate)

    left = jnp.concatenate([lt2[t] for t in range(NZ)], axis=0)
    wide = jnp.concatenate([jnp.where(low64, left, 0.0), jnp.where(low64, 0.0, left)], axis=0)
    gram = lax.dot_general(wide, wide, NT, precision=lax.Precision.HIGHEST, preferred_element_type=F32)
    gram = jnp.where(low64, gram[0:RANK], gram[RANK:])
    gp[0] = gram[0:32]
    gp[1] = gram[32:64]
    copy = send(gp.at[oc], cpair, c0_ss, c0_rs, mate)
    copy.wait_recv()
    sent.append(copy)
    chip = y_hi * NX + x
    c1[chip] = gp[c] + cpair[...]
    for i, (dx, over) in enumerate(far):
        dev = device(at_x(dx), cross if over else y, z, c)
        sent.append(send(c1.at[chip], c1.at[chip], c1_ss.at[i], c1_rs.at[i], dev))
    for i, (dx, over) in enumerate(far):
        arrival(c1.at[lax.div(slots[i], NC)], c1_ss.at[i], c1_rs.at[i], mate)
    total = c1[0]
    for t in range(1, 8):
        total = total + c1[t]
    cfull[c] = total
    copy = send(cfull.at[c], cfull.at[c], c2_ss, c2_rs, mate)
    arrival(cfull.at[oc], c2_ss, c2_rs, mate)
    sent.append(copy)
    gram = jnp.concatenate([cfull[0], cfull[1]], axis=0)

    key_rows, val_rows = solve_rows(gram, left)
    obl[0] = key_rows.astype(BF16)
    obl[1] = val_rows.astype(BF16)
    store_o = pltpu.make_async_copy(obl, o_out, out_sem.at[1])
    store_o.start()

    ordered = jnp.concatenate([obl[oc], obl[c]], axis=0)
    firsts = (x, y)
    seconds = (y, x)
    ds = (2, 1, 3, 0)

    def first(pq, d):
        return lax.rem(firsts[pq] + d, 4)

    def second(pq, d):
        return lax.rem(seconds[pq] + d, 4)

    def dev1(pq, d):
        return device(at_x(d), y, z, c) if pq == 0 else device(x, at_y(d), z, c)

    def dev2(pq, d):
        return device(x, at_y(d), z, c) if pq == 0 else device(at_x(d), y, z, c)

    pair_copies = {}
    for k, d in enumerate(ds):
        for pq in range(2):
            i1 = first(pq, d)
            for h in range(2):
                term = lax.dot_general(
                    ordered, mbuf[pq * 8 + i1 * 2 + h], NN, preferred_element_type=F32
                )
                for i in range(2):
                    for a in range(4):
                        for b in range(2):
                            cols = slice(i * 256 + b * 128, i * 256 + b * 128 + 128)
                            obuf[pq, i1, 2 * h + i, 2 * a + b] = term[16 * a : 16 * a + 16, cols].astype(BF16)
                            wbuf[pq, i1, 2 * h + i, 2 * a + b] = term[64 + 16 * a : 80 + 16 * a, cols]
            pair_copies[pq, k] = send(
                obuf.at[pq, i1], pr.at[pq, i1], e0_ss.at[pq, k], e0_rs.at[pq, k], mate
            )
    for k, d in enumerate(ds):
        for pq in range(2):
            i1 = first(pq, d)
            pair_copies[pq, k].wait_recv()
            sent.append(pair_copies[pq, k])
            total = wbuf[pq, i1] + pr[pq, i1].astype(F32)
            if d == 0:
                wbuf[pq, i1] = total
            else:
                s1[pq, k] = total.astype(BF16)
                sent.append(
                    send(s1.at[pq, k], r2.at[pq, k], e1_ss.at[pq, k], e1_rs.at[pq, k], dev1(pq, d))
                )
    for pq in range(2):
        for k in range(3):
            arrival(r2.at[pq, k], e1_ss.at[pq, k], e1_rs.at[pq, k], mate)
        i1 = first(pq, 0)
        for k, d in enumerate(ds):
            i2 = second(pq, d)
            total = wbuf[pq, i1, i2]
            for t in range(3):
                total = total + r2[pq, t, i2].astype(F32)
            if d == 0:
                wbuf[pq, i1, i2] = total
            else:
                s2[pq, k] = total.astype(BF16)
                sent.append(
                    send(s2.at[pq, k], r3.at[pq, k], e2_ss.at[pq, k], e2_rs.at[pq, k], dev2(pq, d))
                )
    for pq in range(2):
        for k in range(3):
            arrival(r3.at[pq, k], e2_ss.at[pq, k], e2_rs.at[pq, k], mate)
        i1, i2 = first(pq, 0), second(pq, 0)
        total = wbuf[pq, i1, i2]
        for t in range(3):
            total = total + r3[pq, t].astype(F32)
        wbuf[pq, i1, i2] = total
        s3[:, pq] = total.astype(BF16)
    for i, dz in enumerate(zs):
        there = at_z(dz)
        sent.append(send(s3.at[there], r4.at[i], e3_ss.at[i], e3_rs.at[i], device(x, y, there, c)))
    for i in range(7):
        arrival(r4.at[i], e3_ss.at[i], e3_rs.at[i], mate)
    for pq in range(2):
        i1, i2 = first(pq, 0), second(pq, 0)
        total = wbuf[pq, i1, i2, z]
        for i in range(7):
            total = total + r4[i, pq].astype(F32)
        fbuf[c, pq, i1, i2, z] = (total / REPLICAS).astype(BF16)

    for pq in range(2):
        piece = fbuf.at[c, pq, first(pq, 0), second(pq, 0), z]
        for i, dz in enumerate(zs):
            sent.append(send(piece, piece, g3_ss.at[pq, i], g3_rs.at[pq, i], device(x, y, at_z(dz), c)))
    for pq in range(2):
        i1, i2 = first(pq, 0), second(pq, 0)
        for i, dz in enumerate(zs):
            arrival(fbuf.at[c, pq, i1, i2, lax.rem(z + NZ - dz, NZ)], g3_ss.at[pq, i], g3_rs.at[pq, i], mate)
        piece = fbuf.at[c, pq, i1, i2]
        for k in range(3):
            sent.append(send(piece, piece, g2_ss.at[pq, k], g2_rs.at[pq, k], dev2(pq, ds[k])))
    for pq in range(2):
        i1 = first(pq, 0)
        for k in range(3):
            arrival(fbuf.at[c, pq, i1, second(pq, 4 - ds[k])], g2_ss.at[pq, k], g2_rs.at[pq, k], mate)
        piece = fbuf.at[c, pq, i1]
        for k in range(3):
            sent.append(send(piece, piece, g1_ss.at[pq, k], g1_rs.at[pq, k], dev1(pq, ds[k])))
        sent.append(send(piece, piece, g0_ss.at[pq, 3], g0_rs.at[pq, 3], mate))
    stores = []
    for k in (1, 2, 0):
        for pq in range(2):
            piece = fbuf.at[c, pq, first(pq, 4 - ds[k])]
            arrival(piece, g1_ss.at[pq, k], g1_rs.at[pq, k], mate)
            sent.append(send(piece, piece, g0_ss.at[pq, k], g0_rs.at[pq, k], mate))
    stores.append(pltpu.make_async_copy(fbuf.at[c], f_out.at[c], out_sem.at[2]))
    stores[-1].start()
    for k in (3, 1, 2, 0):
        for pq in range(2):
            piece = fbuf.at[oc, pq, first(pq, 4 - ds[k])]
            arrival(piece, g0_ss.at[pq, k], g0_rs.at[pq, k], mate)
    stores.append(pltpu.make_async_copy(fbuf.at[oc], f_out.at[oc], out_sem.at[3]))
    stores[-1].start()
    for copy in stores:
        copy.wait()
    store_m.wait()
    store_o.wait()
    for copy in sent:
        copy.wait_send()


def out_kernel(m_ref, o_ref, f_ref, uk, nk, uv, nv, fk, fv):
    s = lax.axis_index("shard")
    whole = jnp.concatenate([o_ref[0], o_ref[1]], axis=0)
    for i in range(4):
        sides = []
        for m in range(2):
            rows = [
                jnp.concatenate([f_ref[m, 0, 0, i, 2 * a], f_ref[m, 0, 0, i, 2 * a + 1]], axis=1)
                for a in range(4)
            ]
            sides.append(jnp.concatenate(rows, axis=0))
        factor = jnp.concatenate(sides, axis=0)
        approx = lax.dot_general(whole, factor, (((0,), (0,)), ((), ())), preferred_element_type=F32)
        cols = slice(256 * i, 256 * i + 256)
        merged = m_ref[i // 2, :, 256 * (i % 2) : 256 * (i % 2) + 256].astype(F32)
        rest = (merged - approx).astype(BF16)
        approx = approx.astype(BF16)
        uk[:, cols] = approx[:ROWS]
        uv[:, cols] = approx[ROWS:]
        nk[0, :, cols] = rest[:ROWS]
        nv[0, :, cols] = rest[ROWS:]

        @pl.when(jnp.logical_and(pl.program_id(0) == lax.div(s, 2), lax.rem(s, 2) == i // 2))
        def _():
            half = slice(256 * (i % 2), 256 * (i % 2) + 256)
            fk[:, half] = sides[0].astype(F32)
            fv[:, half] = sides[1].astype(F32)


def per_device(grad_key, error_key, prev_key, grad_val, error_val, prev_val):
    vm = pltpu.VMEM
    dma = pltpu.SemaphoreType.DMA
    scratch = [
        vm((2, ROWS, 8192), BF16), vm((2, ROWS, 8192), BF16),
        vm((BLKS, 128, BLK), BF16), vm((BLKS, 128, BLK), BF16),
        vm((128, 128), F32), vm((8, 8, 128), F32), vm((16, 8, 128), F32), vm((8, 8, 128), F32),
        vm((2, 32, 128), F32), vm((32, 128), F32), vm((8, 32, 128), F32), vm((2, 32, 128), F32),
        vm((2, RANK, 128), BF16),
        vm((2, 4, 4, 8, 16, 128), BF16), vm((2, 4, 4, 8, 16, 128), F32), vm((2, 4, 4, 8, 16, 128), BF16),
        vm((2, 3, 4, 8, 16, 128), BF16), vm((2, 3, 4, 8, 16, 128), BF16),
        vm((2, 3, 8, 16, 128), BF16), vm((2, 3, 8, 16, 128), BF16),
        vm((8, 2, 16, 128), BF16), vm((7, 2, 16, 128), BF16),
        vm((2, 2, 4, 4, 8, 16, 128), BF16),
        dma((6,)), dma((4,)),
    ]
    for n in ((7,), (8,), (15,), (7,), None, (7,), None, (2, 4), (2, 3), (2, 3), (7,), (2, 7), (2, 3), (2, 3), (2, 4)):
        for _ in range(2):
            scratch.append(dma if n is None else dma(n))
    hbm = pl.BlockSpec(memory_space=pl.ANY)
    merged, ortho, factor = pl.pallas_call(
        step_kernel,
        name="exchange",
        out_shape=(
            jax.ShapeDtypeStruct((BLKS, 128, BLK), BF16),
            jax.ShapeDtypeStruct((2, RANK, 128), BF16),
            jax.ShapeDtypeStruct((2, 2, 4, 4, 8, 16, 128), BF16),
        ),
        in_specs=[hbm] * 6,
        out_specs=(hbm, hbm, hbm),
        scratch_shapes=scratch,
        compiler_params=pltpu.CompilerParams(
            collective_id=0, has_side_effects=True, vmem_limit_bytes=40 * 2**20
        ),
    )(grad_key, error_key, prev_key.T, grad_val, error_val, prev_val.T)

    def rows(shape):
        return pl.BlockSpec(shape, lambda i: (0, i) if len(shape) == 2 else (0, 0, i))

    uk, nk, uv, nv, fk, fv = pl.pallas_call(
        out_kernel,
        name="outputs",
        grid=(8,),
        out_shape=(
            jax.ShapeDtypeStruct((ROWS, 8192), BF16), jax.ShapeDtypeStruct((1, ROWS, 8192), BF16),
            jax.ShapeDtypeStruct((ROWS, 8192), BF16), jax.ShapeDtypeStruct((1, ROWS, 8192), BF16),
            jax.ShapeDtypeStruct((RANK, BLK), F32), jax.ShapeDtypeStruct((RANK, BLK), F32),
        ),
        in_specs=[
            pl.BlockSpec((2, 128, BLK), lambda i: (i, 0, 0)),
            pl.BlockSpec((2, RANK, 128), lambda i: (0, 0, 0)),
            pl.BlockSpec((2, 1, 1, 4, 8, 16, 128), lambda i: (0, i // 4, i % 4, 0, 0, 0, 0)),
        ],
        out_specs=(
            rows((ROWS, 1024)), rows((1, ROWS, 1024)), rows((ROWS, 1024)), rows((1, ROWS, 1024)),
            pl.BlockSpec((RANK, BLK), lambda i: (0, 0)), pl.BlockSpec((RANK, BLK), lambda i: (0, 0)),
        ),
    )(merged, ortho, factor)
    return uk, nk, fk.T, uv, nv, fv.T


def solution(mesh):
    wide = P("replica", "shard", None)
    flat = P("shard", None)
    return jax.shard_map(
        per_device,
        mesh=mesh,
        in_specs=(wide, wide, flat, wide, wide, flat),
        out_specs=(flat, wide, flat, flat, wide, flat),
        check_vma=False,
    )
```

time: 557 us -> 108 us (0.19)
  waiting for transfers between devices: 373 us -> 0 us
  blocking collectives: 122 us -> 0 us
  Pallas kernels: 0 us -> 97.4 us
  other arithmetic: 25.7 us -> 0 us
  matrix products: 15.5 us -> 0 us
  between operations: 15.2 us -> 0.67 us
  local copies, waits for them, and re-layouts: 3.97 us -> 9.82 us
    psum x1 -> x0, waiting for transfers between devices: 266 us -> none  [expand(): q_whole = lax.psum(q_term, ('replica', 'shard')) / replicas]
    psum x2 -> x0, blocking collectives: 122 us -> none  [the longest x1 73.4 us: project(): gram = lax.psum(gram_of(left), 'shard')]
    all_gather x2 -> x0, waiting for transfers between devices: 106 us -> none  [project(): gathered = lax.all_gather(previous, 'shard', axis=0, tiled=True)]
    pallas_call x0 -> x2, Pallas kernels: none -> 97.4 us  [the longest x1 88.1 us: per_device(): pl.pallas_call(step_kernel, name='exchange', out_shape=(jax.ShapeDtypeStr...]
    another operation x10 -> x0, other arithmetic: 24.1 us -> none  [the longest x6 13 us: orthonormal(): lower = jnp.linalg.cholesky(ridged)]
    dot_general x8 -> x0, matrix products: 15 us -> none  [the longest x2 5.49 us: expand(): jnp.einsum('nk,ck->nc', ortho_b, factor_b, preferred_element_type=jnp.flo...]
    unnamed x12 -> x18, local copies, waits for them, and re-layouts: 2.49 us -> 9.82 us
  transfers between devices with their start and end apart: 3 -> 0, of which waited for: 3 -> 0; matrix products, arithmetic and copies ran while one was open for 0% -> 0% of each run, Pallas kernels for 0% -> 0%
where the time goes in v1:
time: 108 us
  Pallas kernels  97.4 us (90%)
  local copies, waits for them, and re-layouts  9.82 us (9%)
    pallas_call x1, Pallas kernels, per_device(): pl.pallas_call(step_kernel, name='exchange', out_shape=(jax.ShapeDtypeStr...  88.1 us
    unnamed x18, local copies, waits for them, and re-layouts  9.82 us
    pallas_call x1, Pallas kernels, per_device(): pl.pallas_call(out_kernel, name='outputs', grid=(8,), out_shape=(jax.Shap...  9.32 us

profile of v1, /device:TPU:1, one launch (start us, length us, event | category | flops | bytes accessed | tf_op | source)
XLA Modules:
  0.0 107.9 jit_solution(18060204613338863164)
XLA Ops:
  0.6 0.0 copy-start.2
  0.6 1.2 %copy-done.2 = bf16[1,64,8192]{2,1,0:T(8,128)(2,1)S(1)} copy-done((bf16[1,64,8192]{2,1,0:T(8,128)(2,1)S(1)}, bf16[1,64,8192]{2,1,0:T(8,128)(2,1)}, u32[]{:S(2)}) %copy-start.2) | copy-done | bytes 1048600
  1.9 0.0 copy-start.3
  1.9 1.2 %copy-done.3 = bf16[1,64,8192]{2,1,0:T(8,128)(2,1)S(1)} copy-done((bf16[1,64,8192]{2,1,0:T(8,128)(2,1)S(1)}, bf16[1,64,8192]{2,1,0:T(8,128)(2,1)}, u32[]{:S(2)}) %copy-start.3) | copy-done | bytes 1048600
  3.1 0.0 copy-start.4
  3.1 1.2 %copy-done.4 = bf16[1,64,8192]{2,1,0:T(8,128)(2,1)S(1)} copy-done((bf16[1,64,8192]{2,1,0:T(8,128)(2,1)S(1)}, bf16[1,64,8192]{2,1,0:T(8,128)(2,1)}, u32[]{:S(2)}) %copy-start.4) | copy-done | bytes 1048600
  4.3 0.0 copy-start.5
  4.3 1.2 %copy-done.5 = bf16[1,64,8192]{2,1,0:T(8,128)(2,1)S(1)} copy-done((bf16[1,64,8192]{2,1,0:T(8,128)(2,1)S(1)}, bf16[1,64,8192]{2,1,0:T(8,128)(2,1)}, u32[]{:S(2)}) %copy-start.5) | copy-done | bytes 1048600
  5.5 0.0 copy-start.6
  5.5 0.8 copy-done.6
  6.4 0.0 copy-start.7
  6.4 0.8 copy-done.7
  7.2 88.1 %exchange.1 = (bf16[16,128,512]{2,1,0:T(8,128)(2,1)S(1)}, bf16[2,64,128]{2,1,0:T(8,128)(2,1)S(1)}, bf16[2,2,4,4,8,16,128]{6,5,4,3,2,1,0:T(8,128)(2,1)S(1)}) custom-call(bf16[1,64,8192]{2,1,0:T(8,128)(2,1)S(1)} %copy-done.2, bf16[1,64,8192]{2,1,0:T(8,128)(2,1)S(1)} %copy-done.3, bf16[64,512]{1,0:T(8,128)(2,1)S(1)} %bitcast.4, ...), custom_call_target="tpu_custom_call" | custom-call | tf_op jit(solution)/shard_map/exchange/pallas_call | solution.py:408
  95.3 0.0 copy-start
  95.3 1.3 %copy-done = bf16[16,128,512]{2,1,0:T(8,128)(2,1)} copy-done((bf16[16,128,512]{2,1,0:T(8,128)(2,1)}, bf16[16,128,512]{2,1,0:T(8,128)(2,1)S(1)}, u32[]{:S(2)}) %copy-start) | copy-done | bytes 2097176
  96.6 0.0 copy-start.1
  96.6 1.3 %copy-done.1 = bf16[2,2,4,4,8,16,128]{6,5,4,3,2,1,0:T(8,128)(2,1)} copy-done((bf16[2,2,4,4,8,16,128]{6,5,4,3,2,1,0:T(8,128)(2,1)}, bf16[2,2,4,4,8,16,128]{6,5,4,3,2,1,0:T(8,128)(2,1)S(1)}, u32[]{:S(2)}) %copy-start.1) | copy-done | bytes 2097176
  97.9 0.0 copy-start.8
  97.9 0.6 copy-done.8
  98.5 9.3 %outputs.1 = (bf16[64,8192]{1,0:T(8,128)(2,1)}, bf16[1,64,8192]{2,1,0:T(8,128)(2,1)}, bf16[64,8192]{1,0:T(8,128)(2,1)}, bf16[1,64,8192]{2,1,0:T(8,128)(2,1)}, f32[64,512]{1,0:T(8,128)}, /*index=5*/f32[64,512]{1,0:T(8,128)}) custom-call(bf16[16,128,512]{2,1,0:T(8,128)(2,1)} %copy-done, bf16[2,64,128]{2,1,0:T(8,128)(2,1)} %copy-done.8, ...), custom_call_target="tpu_custom_call" | custom-call | tf_op jit(solution)/shard_map/outputs/pallas_call | solution.py:427
Async XLA Ops:
  0.6 1.2 %copy-start.2 = (bf16[1,64,8192]{2,1,0:T(8,128)(2,1)S(1)}, bf16[1,64,8192]{2,1,0:T(8,128)(2,1)}, u32[]{:S(2)}) copy-start(bf16[1,64,8192]{2,1,0:T(8,128)(2,1)} %gk.1) | copy-start | bytes 3145732
  1.9 1.2 %copy-start.3 = (bf16[1,64,8192]{2,1,0:T(8,128)(2,1)S(1)}, bf16[1,64,8192]{2,1,0:T(8,128)(2,1)}, u32[]{:S(2)}) copy-start(bf16[1,64,8192]{2,1,0:T(8,128)(2,1)} %ek.1) | copy-start | bytes 3145732
  3.1 1.2 %copy-start.4 = (bf16[1,64,8192]{2,1,0:T(8,128)(2,1)S(1)}, bf16[1,64,8192]{2,1,0:T(8,128)(2,1)}, u32[]{:S(2)}) copy-start(bf16[1,64,8192]{2,1,0:T(8,128)(2,1)} %gv.1) | copy-start | bytes 3145732
  4.3 1.2 %copy-start.5 = (bf16[1,64,8192]{2,1,0:T(8,128)(2,1)S(1)}, bf16[1,64,8192]{2,1,0:T(8,128)(2,1)}, u32[]{:S(2)}) copy-start(bf16[1,64,8192]{2,1,0:T(8,128)(2,1)} %ev.1) | copy-start | bytes 3145732
  5.5 0.8 copy-start.6
  6.4 0.8 copy-start.7
  95.3 1.3 %copy-start = (bf16[16,128,512]{2,1,0:T(8,128)(2,1)}, bf16[16,128,512]{2,1,0:T(8,128)(2,1)S(1)}, u32[]{:S(2)}) copy-start(bf16[16,128,512]{2,1,0:T(8,128)(2,1)S(1)} %get-tuple-element.15.m_ref) | copy-start | bytes 6291460
  96.6 1.3 %copy-start.1 = (bf16[2,2,4,4,8,16,128]{6,5,4,3,2,1,0:T(8,128)(2,1)}, bf16[2,2,4,4,8,16,128]{6,5,4,3,2,1,0:T(8,128)(2,1)S(1)}, u32[]{:S(2)}) copy-start(bf16[2,2,4,4,8,16,128]{6,5,4,3,2,1,0:T(8,128)(2,1)S(1)} %get-tuple-element.17.f_ref) | copy-start | bytes 6291460
  97.9 0.6 copy-start.8

commit v2 on v1

v2 whole, which is shorter than its diff:
```python
import functools

import jax
import jax.numpy as jnp
from jax import lax
from jax.experimental import pallas as pl
from jax.experimental.pallas import tpu as pltpu
from jax.sharding import PartitionSpec as P

MESH = pl.DeviceIdType.MESH
F32, BF16 = jnp.float32, jnp.bfloat16
NX, NY, NZ, NC = 4, 4, 8, 2
REPLICAS = 16
RANK = 64
ROWS = 64
BLK = 512
BLKS = 16
COL = 256
COLS = 32
RIDGE = 1e-6
NT = (((1,), (1,)), ((), ()))
NN = (((1,), (0,)), ((), ()))


def device(x, y, z, c):
    return (lax.rem(y, 2) * NZ + z, (lax.div(y, 2) * NX + x) * NC + c)


def send(src, dst, ssem, rsem, dev):
    copy = pltpu.make_async_remote_copy(
        src_ref=src, dst_ref=dst, send_sem=ssem, recv_sem=rsem, device_id=dev, device_id_type=MESH
    )
    copy.start()
    return copy


def arrival(dst, ssem, rsem, dev):
    pltpu.make_async_remote_copy(
        src_ref=dst, dst_ref=dst, send_sem=ssem, recv_sem=rsem, device_id=dev, device_id_type=MESH
    ).wait_recv()


def lanes_low(shape):
    return lax.broadcasted_iota(jnp.int32, shape, 1) < RANK


def solve_rows(gram, left):
    shape = (RANK, 128)
    row = lax.broadcasted_iota(jnp.int32, shape, 0)
    lane = lax.broadcasted_iota(jnp.int32, shape, 1)
    low = lane < RANK
    swapped = pltpu.roll(left, RANK, 1)
    out = []
    for side in range(2):
        here = low if side == 0 else jnp.logical_not(low)
        diag = lane == row + side * RANK
        trace = jnp.sum(jnp.where(diag, gram, 0.0))
        ridge = RIDGE * (trace / RANK)
        whole = jnp.where(here, gram + jnp.where(diag, ridge, 0.0), swapped)
        out.append([whole[8 * t : 8 * t + 8] for t in range(8)])
    sub = lax.broadcasted_iota(jnp.int32, (8, 128), 0)
    for j in range(RANK - 1):
        top, pos = divmod(j, 8)
        for side in range(2):
            tiles = out[side]
            col = side * RANK + j
            pivot_row = tiles[top][pos : pos + 1, :]
            inv = 1.0 / pivot_row[:, col : col + 1]
            scaled = pivot_row * inv
            for t in range(top, 8):
                if t == top:
                    if pos == 7:
                        continue
                    factor = jnp.where(sub > pos, jnp.broadcast_to(tiles[t][:, col : col + 1], (8, 128)), 0.0)
                else:
                    factor = tiles[t][:, col : col + 1]
                tiles[t] = tiles[t] - factor * scaled
    done = []
    for side in range(2):
        whole = jnp.concatenate(out[side], axis=0)
        diag = lane == row + side * RANK
        pivots = jnp.sum(jnp.where(diag, whole, 0.0), axis=1, keepdims=True)
        done.append(pltpu.roll(whole * lax.rsqrt(pivots), RANK, 1))
    return jnp.where(low, done[0], 0.0), jnp.where(low, 0.0, done[1])


def step_kernel(
    gk, ek, pk, gv, ev, pv,
    uk, nk, fk, uv, nv, fv,
    grads, errors, mbuf, pbuf, acc, lbuf, r1, lt2, gp, cpair, c1, cfull, obl,
    obuf, wbuf, pr, s1, r2, s2, r3, s3, r4, fbuf, fstage,
    load_sem, out_sem, fac_sem,
    a_ss, a_rs, q_ss, q_rs, af_ss, af_rs, b_ss, b_rs, b2_ss, b2_rs, c0_ss, c0_rs, c1_ss, c1_rs, c2_ss, c2_rs,
    e0_ss, e0_rs, e1_ss, e1_rs, e2_ss, e2_rs, e3_ss, e3_rs,
    g3_ss, g3_rs, g2_ss, g2_rs, g1_ss, g1_rs, g0_ss, g0_rs,
):
    r = lax.axis_index("replica")
    s = lax.axis_index("shard")
    y_lo, z = lax.div(r, NZ), lax.rem(r, NZ)
    y_hi, x, c = lax.div(s, NX * NC), lax.rem(lax.div(s, NC), NX), lax.rem(s, NC)
    y = 2 * y_hi + y_lo
    oc = 1 - c
    cross = lax.rem(y + 3 + 2 * y_lo, NY)
    flip = 2 * y_hi + 1 - y_lo
    mate = device(x, y, z, oc)

    def at_x(d):
        return lax.rem(x + d, NX)

    def at_y(d):
        return lax.rem(y + d, NY)

    def at_z(d):
        return lax.rem(z + d, NZ)

    own_prev = [
        pltpu.make_async_copy(pk, pbuf.at[s, pl.ds(0, RANK)], load_sem.at[4]),
        pltpu.make_async_copy(pv, pbuf.at[s, pl.ds(RANK, RANK)], load_sem.at[5]),
    ]
    loads = [
        pltpu.make_async_copy(gk.at[0], grads.at[0], load_sem.at[0]),
        pltpu.make_async_copy(ek.at[0], errors.at[0], load_sem.at[1]),
        pltpu.make_async_copy(gv.at[0], grads.at[1], load_sem.at[2]),
        pltpu.make_async_copy(ev.at[0], errors.at[1], load_sem.at[3]),
    ]
    partners = [device(x, flip, at_z(d), c) for d in (4, 3, 5, 2, 6, 1, 7)]
    partners += [device(x, y, at_z(d), c) for d in (4, 3, 5, 2, 6, 1, 7)]
    partners += [device(at_x(d), cross, z, c) for d in (2, 1, 3)]
    partners += [device(at_x(d), y, z, c) for d in (2, 1, 3)]
    partners += [device(x, at_y(d), z, c) for d in (2, 1, 3)]
    partners += [mate]
    barrier = pltpu.get_barrier_semaphore()
    for dev in partners:
        pl.semaphore_signal(barrier, inc=1, device_id=dev, device_id_type=MESH)
    for copy in own_prev + loads:
        copy.start()
    for copy in own_prev:
        copy.wait()
    pl.semaphore_wait(barrier, len(partners))

    sent = []

    far = [(2, 1), (1, 1), (3, 1), (2, 0), (1, 0), (3, 0), (0, 1)]

    def quarter(slot, q):
        return pbuf.at[slot, pl.ds(pl.multiple_of(lax.rem(q, 4) * 32, 32), 32)]

    color = z + 2 * y_lo
    for i, (dx, over) in enumerate(far):
        dev = device(at_x(dx), cross if over else y, z, c)
        piece = quarter(s, color + 2 * over)
        sent.append(send(piece, piece, a_ss.at[i], a_rs.at[i], dev))
    sent.append(send(pbuf.at[s], pbuf.at[s], af_ss.at[7], af_rs.at[7], mate))
    near = (device(x, flip, z, c), device(x, y, at_z(1), c), device(x, y, at_z(7), c))

    for copy in loads:
        copy.wait()

    def merge(b, carry):
        cols = pl.ds(pl.multiple_of(b * COL, COL), COL)
        for m in range(2):
            total = grads[m, :, cols].astype(F32) + errors[m, :, cols].astype(F32)
            mbuf[b, m * ROWS : (m + 1) * ROWS, :] = total.astype(BF16)
        return carry

    lax.fori_loop(0, COLS, merge, 0)

    def left_term(slot):
        low = lax.dot_general(pbuf[slot, :, 0:COL], mbuf[2 * slot], NT, preferred_element_type=F32)
        high = lax.dot_general(pbuf[slot, :, COL:], mbuf[2 * slot + 1], NT, preferred_element_type=F32)
        return low + high

    acc[...] = left_term(s)
    order = (4, 5, 6, 1, 2, 3, 0)
    slots = []
    for i, (dx, over) in enumerate(far):
        yy = (1 - y_hi) if over else y_hi
        slots.append((yy * NX + lax.rem(x + NX - dx, NX)) * NC)
    for i in order:
        piece = quarter(slots[i] + c, color)
        arrival(piece, a_ss.at[i], a_rs.at[i], mate)
        for n in range(3):
            sent.append(send(piece, piece, q_ss.at[i, n], q_rs.at[i, n], near[n]))
    for i in order:
        slot = slots[i] + c
        for n in range(3):
            arrival(quarter(slot, color + (2, 3, 1)[n]), q_ss.at[i, n], q_rs.at[i, n], mate)
        sent.append(send(pbuf.at[slot], pbuf.at[slot], af_ss.at[i], af_rs.at[i], mate))
        acc[...] += left_term(slot)
    for i in (7,) + order:
        slot = (s + oc - c) if i == 7 else slots[i] + oc
        arrival(pbuf.at[slot], af_ss.at[i], af_rs.at[i], mate)
        acc[...] += left_term(slot)

    low64 = lanes_low((RANK, 128))
    part = jnp.where(low64, acc[0:RANK, :], acc[RANK:, :])
    for t in range(NZ):
        lbuf[t] = part[8 * t : 8 * t + 8]
    r1[r] = lbuf[z]
    peers = [(1, d) for d in (4, 3, 5, 2, 6, 1, 7, 0)] + [(0, d) for d in (4, 3, 5, 2, 6, 1, 7)]
    for i, (over, dz) in enumerate(peers):
        dev = device(x, flip if over else y, at_z(dz), c)
        sent.append(send(lbuf.at[at_z(dz)], r1.at[r], b_ss.at[i], b_rs.at[i], dev))
    for i, (over, dz) in enumerate(peers):
        slot = ((1 - y_lo) if over else y_lo) * NZ + lax.rem(z + NZ - dz, NZ)
        arrival(r1.at[slot], b_ss.at[i], b_rs.at[i], mate)
    total = r1[0]
    for t in range(1, REPLICAS):
        total = total + r1[t]
    lt2[z] = total / REPLICAS
    zs = (4, 3, 5, 2, 6, 1, 7)
    for i, dz in enumerate(zs):
        sent.append(send(lt2.at[z], lt2.at[z], b2_ss.at[i], b2_rs.at[i], device(x, y, at_z(dz), c)))
    for i, dz in enumerate(zs):
        arrival(lt2.at[lax.rem(z + NZ - dz, NZ)], b2_ss.at[i], b2_rs.at[i], mate)

    left = jnp.concatenate([lt2[t] for t in range(NZ)], axis=0)
    wide = jnp.concatenate([jnp.where(low64, left, 0.0), jnp.where(low64, 0.0, left)], axis=0)
    gram = lax.dot_general(wide, wide, NT, precision=lax.Precision.HIGHEST, preferred_element_type=F32)
    gram = jnp.where(low64, gram[0:RANK], gram[RANK:])
    gp[0] = gram[0:32]
    gp[1] = gram[32:64]
    copy = send(gp.at[oc], cpair, c0_ss, c0_rs, mate)
    copy.wait_recv()
    sent.append(copy)
    chip = y_hi * NX + x
    c1[chip] = gp[c] + cpair[...]
    for i, (dx, over) in enumerate(far):
        dev = device(at_x(dx), cross if over else y, z, c)
        sent.append(send(c1.at[chip], c1.at[chip], c1_ss.at[i], c1_rs.at[i], dev))
    for i, (dx, over) in enumerate(far):
        arrival(c1.at[lax.div(slots[i], NC)], c1_ss.at[i], c1_rs.at[i], mate)
    total = c1[0]
    for t in range(1, 8):
        total = total + c1[t]
    cfull[c] = total
    copy = send(cfull.at[c], cfull.at[c], c2_ss, c2_rs, mate)
    arrival(cfull.at[oc], c2_ss, c2_rs, mate)
    sent.append(copy)
    gram = jnp.concatenate([cfull[0], cfull[1]], axis=0)

    key_rows, val_rows = solve_rows(gram, left)
    obl[0] = key_rows
    obl[1] = val_rows

    ordered = jnp.concatenate([obl[oc], obl[c]], axis=0).astype(BF16)
    firsts = (x, y)
    seconds = (y, x)
    ds = (2, 1, 3, 0)

    def first(pq, d):
        return lax.rem(firsts[pq] + d, 4)

    def second(pq, d):
        return lax.rem(seconds[pq] + d, 4)

    def dev1(pq, d):
        return device(at_x(d), y, z, c) if pq == 0 else device(x, at_y(d), z, c)

    def dev2(pq, d):
        return device(x, at_y(d), z, c) if pq == 0 else device(at_x(d), y, z, c)

    pair_copies = {}
    for j, dj in enumerate(ds):
        for pq in range(2):
            i2 = second(pq, dj)
            for i1 in range(4):
                term = lax.dot_general(ordered, mbuf[pq * 16 + i1 * 4 + i2], NN, preferred_element_type=F32)
                for a in range(4):
                    for b in range(2):
                        cols = slice(b * 128, b * 128 + 128)
                        obuf[pq, i2, i1, 2 * a + b] = term[16 * a : 16 * a + 16, cols].astype(BF16)
                        wbuf[pq, i2, i1, 2 * a + b] = term[64 + 16 * a : 80 + 16 * a, cols]
            pair_copies[pq, j] = send(
                obuf.at[pq, i2], pr.at[pq, i2], e0_ss.at[pq, j], e0_rs.at[pq, j], mate
            )
    for j, dj in enumerate(ds):
        for pq in range(2):
            i2 = second(pq, dj)
            pair_copies[pq, j].wait_recv()
            sent.append(pair_copies[pq, j])
            for k, dk in enumerate(ds):
                i1 = first(pq, dk)
                total = wbuf[pq, i2, i1] + pr[pq, i2, i1].astype(F32)
                if dk == 0:
                    wbuf[pq, i2, i1] = total
                else:
                    s1[pq, j, k] = total.astype(BF16)
                    sent.append(
                        send(s1.at[pq, j, k], r2.at[pq, j, k], e1_ss.at[pq, j, k], e1_rs.at[pq, j, k], dev1(pq, dk))
                    )
    for j, dj in enumerate(ds):
        for pq in range(2):
            i1, i2 = first(pq, 0), second(pq, dj)
            total = wbuf[pq, i2, i1]
            for k in range(3):
                arrival(r2.at[pq, j, k], e1_ss.at[pq, j, k], e1_rs.at[pq, j, k], mate)
                total = total + r2[pq, j, k].astype(F32)
            if dj == 0:
                wbuf[pq, i2, i1] = total
            else:
                s2[pq, j] = total.astype(BF16)
                sent.append(
                    send(s2.at[pq, j], r3.at[pq, j], e2_ss.at[pq, j], e2_rs.at[pq, j], dev2(pq, dj))
                )
    for pq in range(2):
        i1, i2 = first(pq, 0), second(pq, 0)
        total = wbuf[pq, i2, i1]
        for j in range(3):
            arrival(r3.at[pq, j], e2_ss.at[pq, j], e2_rs.at[pq, j], mate)
            total = total + r3[pq, j].astype(F32)
        wbuf[pq, i2, i1] = total
        s3[:, pq] = total.astype(BF16)
    for i, dz in enumerate(zs):
        there = at_z(dz)
        sent.append(send(s3.at[there], r4.at[i], e3_ss.at[i], e3_rs.at[i], device(x, y, there, c)))
    for i in range(7):
        arrival(r4.at[i], e3_ss.at[i], e3_rs.at[i], mate)
    for pq in range(2):
        i1, i2 = first(pq, 0), second(pq, 0)
        total = wbuf[pq, i2, i1, z]
        for i in range(7):
            total = total + r4[i, pq].astype(F32)
        fbuf[c, pq, i1, i2, z] = (total / REPLICAS).astype(BF16)

    for pq in range(2):
        piece = fbuf.at[c, pq, first(pq, 0), second(pq, 0), z]
        for i, dz in enumerate(zs):
            sent.append(send(piece, piece, g3_ss.at[pq, i], g3_rs.at[pq, i], device(x, y, at_z(dz), c)))
    ortho = jnp.concatenate([obl[0], obl[1]], axis=0).T.astype(BF16)

    def sub_piece(pq, k, j):
        return fbuf.at[c, pq, first(pq, 4 - ds[k]), second(pq, 4 - ds[j])]

    def spread(pq, j):
        piece = sub_piece(pq, 3, j)
        for k in range(3):
            sent.append(send(piece, piece, g1_ss.at[pq, j, k], g1_rs.at[pq, j, k], dev1(pq, ds[k])))

    for pq in range(2):
        piece = sub_piece(pq, 3, 3)
        for i, dz in enumerate(zs):
            arrival(
                fbuf.at[c, pq, first(pq, 0), second(pq, 0), lax.rem(z + NZ - dz, NZ)],
                g3_ss.at[pq, i], g3_rs.at[pq, i], mate,
            )
        for k in range(3):
            sent.append(send(piece, piece, g2_ss.at[pq, k], g2_rs.at[pq, k], dev2(pq, ds[k])))
        spread(pq, 3)
    for j in (1, 2, 0):
        for pq in range(2):
            arrival(sub_piece(pq, 3, j), g2_ss.at[pq, j], g2_rs.at[pq, j], mate)
            spread(pq, j)

    stores = []

    def finish(n, pq, k):
        i1 = first(pq, 4 - ds[k])
        arrival(fbuf.at[oc, pq, i1], g0_ss.at[pq, k], g0_rs.at[pq, k], mate)
        at = pl.multiple_of(pq * 4096 + i1 * 1024, 1024)
        for i in range(4):
            sides = []
            for m in range(2):
                rows = [
                    jnp.concatenate([fbuf[m, pq, i1, i, 2 * a], fbuf[m, pq, i1, i, 2 * a + 1]], axis=1)
                    for a in range(4)
                ]
                sides.append(jnp.concatenate(rows, axis=0))
            factor = jnp.concatenate(sides, axis=0)
            approx = lax.dot_general(ortho, factor, NN, preferred_element_type=F32)
            rest = (mbuf[pq * 16 + i1 * 4 + i].astype(F32) - approx).astype(BF16)
            approx = approx.astype(BF16)
            cols = pl.ds(pl.multiple_of(at + i * COL, COL), COL)
            for m in range(2):
                grads[m, :, cols] = approx[m * ROWS : m * ROWS + ROWS]
                errors[m, :, cols] = rest[m * ROWS : m * ROWS + ROWS]
        cols = pl.ds(at, 1024)
        for i, (src, dst) in enumerate(
            (
                (grads.at[0, :, cols], uk.at[:, cols]),
                (errors.at[0, :, cols], nk.at[0, :, cols]),
                (grads.at[1, :, cols], uv.at[:, cols]),
                (errors.at[1, :, cols], nv.at[0, :, cols]),
            )
        ):
            copy = pltpu.make_async_copy(src, dst, out_sem.at[n, i])
            copy.start()
            stores.append(copy)

    pending = None
    for k in (3, 1, 2, 0):
        for pq in range(2):
            if k < 3:
                for j in (3, 1, 2, 0):
                    arrival(sub_piece(pq, k, j), g1_ss.at[pq, j, k], g1_rs.at[pq, j, k], mate)
            piece = fbuf.at[c, pq, first(pq, 4 - ds[k])]
            sent.append(send(piece, piece, g0_ss.at[pq, k], g0_rs.at[pq, k], mate))
            if pending is not None:
                finish(*pending)
            pending = (2 * k + pq, pq, k)
    finish(*pending)
    for i in range(2):
        for m in range(2):
            rows = [
                jnp.concatenate([fbuf[m, s // 8, s % 8 // 2, s % 2 * 2 + i, 2 * a + b] for b in range(2)], axis=1)
                for a in range(4)
            ]
            fstage[m, :, i * COL : (i + 1) * COL] = jnp.concatenate(rows, axis=0).astype(F32)
    for m, dst in enumerate((fk, fv)):
        copy = pltpu.make_async_copy(fstage.at[m], dst, fac_sem.at[m])
        copy.start()
        stores.append(copy)
    for copy in stores:
        copy.wait()
    for copy in sent:
        copy.wait_send()


def per_device(grad_key, error_key, prev_key, grad_val, error_val, prev_val):
    vm = pltpu.VMEM
    dma = pltpu.SemaphoreType.DMA
    scratch = [
        vm((2, ROWS, 8192), BF16), vm((2, ROWS, 8192), BF16),
        vm((COLS, 128, COL), BF16), vm((BLKS, 128, BLK), BF16),
        vm((128, 128), F32), vm((8, 8, 128), F32), vm((16, 8, 128), F32), vm((8, 8, 128), F32),
        vm((2, 32, 128), F32), vm((32, 128), F32), vm((8, 32, 128), F32), vm((2, 32, 128), F32),
        vm((2, RANK, 128), F32),
        vm((2, 4, 4, 8, 16, 128), BF16), vm((2, 4, 4, 8, 16, 128), F32), vm((2, 4, 4, 8, 16, 128), BF16),
        vm((2, 4, 3, 8, 16, 128), BF16), vm((2, 4, 3, 8, 16, 128), BF16),
        vm((2, 3, 8, 16, 128), BF16), vm((2, 3, 8, 16, 128), BF16),
        vm((8, 2, 16, 128), BF16), vm((7, 2, 16, 128), BF16),
        vm((2, 2, 4, 4, 8, 16, 128), BF16), vm((2, RANK, BLK), F32),
        dma((6,)), dma((8, 4)), dma((2,)),
    ]
    for n in (
        (7,), (7, 3), (8,), (15,), (7,), None, (7,), None,
        (2, 4), (2, 4, 3), (2, 3), (7,), (2, 7), (2, 3), (2, 4, 3), (2, 4),
    ):
        for _ in range(2):
            scratch.append(dma if n is None else dma(n))
    hbm = pl.BlockSpec(memory_space=pl.ANY)
    out = pl.BlockSpec(memory_space=pl.ANY)
    update = jax.ShapeDtypeStruct((ROWS, 8192), BF16)
    rest = jax.ShapeDtypeStruct((1, ROWS, 8192), BF16)
    factor = jax.ShapeDtypeStruct((RANK, BLK), F32)
    uk, nk, fk, uv, nv, fv = pl.pallas_call(
        step_kernel,
        name="exchange",
        out_shape=(update, rest, factor, update, rest, factor),
        in_specs=[hbm] * 6,
        out_specs=(out,) * 6,
        scratch_shapes=scratch,
        compiler_params=pltpu.CompilerParams(
            collective_id=0, has_side_effects=True, vmem_limit_bytes=60 * 2**20
        ),
    )(grad_key, error_key, prev_key.T, grad_val, error_val, prev_val.T)
    return uk, nk, fk.T, uv, nv, fv.T


def solution(mesh):
    wide = P("replica", "shard", None)
    flat = P("shard", None)
    return jax.shard_map(
        per_device,
        mesh=mesh,
        in_specs=(wide, wide, flat, wide, wide, flat),
        out_specs=(flat, wide, flat, flat, wide, flat),
        check_vma=False,
    )
```

time: 108 us -> 93.6 us (0.87)
  Pallas kernels: 97.4 us -> 85.5 us
  local copies, waits for them, and re-layouts: 9.82 us -> 7.31 us
    pallas_call x2 -> x1, Pallas kernels: 97.4 us -> 85.5 us  [per_device(): pl.pallas_call(step_kernel, name='exchange', out_shape=(update, rest, fac...]
    unnamed x18 -> x16, local copies, waits for them, and re-layouts: 9.82 us -> 7.31 us
where the time goes in v2:
time: 93.6 us; the launch traced here: 93.4 us
  Pallas kernels  85.5 us (91%)
  local copies, waits for them, and re-layouts  7.31 us (8%)
    pallas_call x1, Pallas kernels, per_device(): pl.pallas_call(step_kernel, name='exchange', out_shape=(update, rest, fac...  85.5 us
    unnamed x16, local copies, waits for them, and re-layouts  7.31 us

profile of v2, /device:TPU:1, one launch (start us, length us, event | category | flops | bytes accessed | tf_op | source)
XLA Modules:
  0.0 93.4 jit_solution(16307469957166654727)
XLA Ops:
  0.6 85.5 %exchange.1 = (bf16[64,8192]{1,0:T(8,128)(2,1)}, bf16[1,64,8192]{2,1,0:T(8,128)(2,1)}, f32[64,512]{1,0:T(8,128)}, bf16[64,8192]{1,0:T(8,128)(2,1)}, bf16[1,64,8192]{2,1,0:T(8,128)(2,1)}, /*index=5*/f32[64,512]{1,0:T(8,128)}) custom-call(bf16[1,64,8192]{2,1,0:T(8,128)(2,1)} %gk.1, bf16[1,64,8192]{2,1,0:T(8,128)(2,1)} %ek.1, bf16[64,512]{1,0:T(8,128)(2,1)} %bitcast.6, ...), custom_call_target="tpu_custom_call" | custom-call | tf_op jit(solution)/shard_map/exchange/pallas_call | solution.py:446
  86.1 0.0 copy-start.2
  86.1 2.4 %copy.18 = bf16[64,8192]{1,0:T(8,128)(2,1)} copy(bf16[64,8192]{1,0:T(8,128)(2,1)} %get-tuple-element.24) | data formatting | bytes 2097152
  88.5 0.0 copy-done.2
  88.5 0.0 copy-start.4
  88.5 0.0 copy-start.1
  88.5 1.0 %copy.19 = bf16[1,64,8192]{2,1,0:T(8,128)(2,1)} copy(bf16[1,64,8192]{2,1,0:T(8,128)(2,1)S(1)} %copy-done.2) | data formatting | bytes 2097152
  89.4 0.0 copy-done.4
  89.5 0.7 copy.20
  90.1 0.0 copy-done.1
  90.1 0.0 copy-start
  90.1 1.0 %copy.21 = bf16[64,8192]{1,0:T(8,128)(2,1)} copy(bf16[64,8192]{1,0:T(8,128)(2,1)S(1)} %copy-done.1) | data formatting | bytes 2097152
  91.1 0.6 copy-done
  91.7 0.0 copy-start.3
  91.7 1.0 %copy.22 = bf16[1,64,8192]{2,1,0:T(8,128)(2,1)} copy(bf16[1,64,8192]{2,1,0:T(8,128)(2,1)S(1)} %copy-done) | data formatting | bytes 2097152
  92.7 0.1 copy-done.3
  92.8 0.7 copy.23
Async XLA Ops:
  86.1 2.4 %copy-start.2 = (bf16[1,64,8192]{2,1,0:T(8,128)(2,1)S(1)}, bf16[1,64,8192]{2,1,0:T(8,128)(2,1)}, u32[]{:S(2)}) copy-start(bf16[1,64,8192]{2,1,0:T(8,128)(2,1)} %get-tuple-element.25) | copy-start | bytes 3145732
  88.5 1.0 %copy-start.4 = (f32[64,512]{1,0:T(8,128)S(1)}, f32[64,512]{1,0:T(8,128)}, u32[]{:S(2)}) copy-start(f32[64,512]{1,0:T(8,128)} %get-tuple-element.14) | copy-start | bytes 393220
  88.5 1.7 %copy-start.1 = (bf16[64,8192]{1,0:T(8,128)(2,1)S(1)}, bf16[64,8192]{1,0:T(8,128)(2,1)}, u32[]{:S(2)}) copy-start(bf16[64,8192]{1,0:T(8,128)(2,1)} %get-tuple-element.27) | copy-start | bytes 3145732
  90.1 1.6 %copy-start = (bf16[1,64,8192]{2,1,0:T(8,128)(2,1)S(1)}, bf16[1,64,8192]{2,1,0:T(8,128)(2,1)}, u32[]{:S(2)}) copy-start(bf16[1,64,8192]{2,1,0:T(8,128)(2,1)} %get-tuple-element.28) | copy-start | bytes 3145732
  91.7 1.0 %copy-start.3 = (f32[64,512]{1,0:T(8,128)S(1)}, f32[64,512]{1,0:T(8,128)}, u32[]{:S(2)}) copy-start(f32[64,512]{1,0:T(8,128)} %get-tuple-element.17) | copy-start | bytes 393220

commit v3 on v2

--- a/solution.py
+++ b/solution.py
@@ -50,38 +50,50 @@
     lane = lax.broadcasted_iota(jnp.int32, shape, 1)
     low = lane < RANK
     swapped = pltpu.roll(left, RANK, 1)
-    out = []
+    rest = []
     for side in range(2):
         here = low if side == 0 else jnp.logical_not(low)
         diag = lane == row + side * RANK
         trace = jnp.sum(jnp.where(diag, gram, 0.0))
         ridge = RIDGE * (trace / RANK)
-        whole = jnp.where(here, gram + jnp.where(diag, ridge, 0.0), swapped)
-        out.append([whole[8 * t : 8 * t + 8] for t in range(8)])
+        rest.append(jnp.where(here, gram + jnp.where(diag, ridge, 0.0), swapped))
     sub = lax.broadcasted_iota(jnp.int32, (8, 128), 0)
-    for j in range(RANK - 1):
-        top, pos = divmod(j, 8)
+    done = [[], []]
+    for t in range(8):
+        count = RANK - 8 * t
+        head = [rest[side][:8] for side in range(2)]
+        tail = [rest[side][8:] if t < 7 else None for side in range(2)]
+        hcol, tcol = [], []
         for side in range(2):
-            tiles = out[side]
-            col = side * RANK + j
-            pivot_row = tiles[top][pos : pos + 1, :]
-            inv = 1.0 / pivot_row[:, col : col + 1]
-            scaled = pivot_row * inv
-            for t in range(top, 8):
-                if t == top:
-                    if pos == 7:
-                        continue
-                    factor = jnp.where(sub > pos, jnp.broadcast_to(tiles[t][:, col : col + 1], (8, 128)), 0.0)
-                else:
-                    factor = tiles[t][:, col : col + 1]
-                tiles[t] = tiles[t] - factor * scaled
-    done = []
+            first = side * RANK + 8 * t
+            cols = [jnp.broadcast_to(rest[side][:, first + k : first + k + 1], (count, 128)) for k in range(8)]
+            hcol.append([col[:8] for col in cols])
+            tcol.append([col[8:] for col in cols] if t < 7 else None)
+        for k in range(8):
+            for side in range(2):
+                inv = 1.0 / hcol[side][k][k : k + 1, :]
+                across = [hcol[side][j][k : k + 1, :] for j in range(8)]
+                pivot = head[side][k : k + 1, :]
+                if k < 7:
+                    m = jnp.where(sub > k, hcol[side][k] * inv, 0.0)
+                    for j in range(k + 1, 8):
+                        hcol[side][j] = hcol[side][j] - m * across[j]
+                    head[side] = head[side] - m * pivot
+                if t < 7:
+                    m = tcol[side][k] * inv
+                    for j in range(k + 1, 8):
+                        tcol[side][j] = tcol[side][j] - m * across[j]
+                    tail[side] = tail[side] - m * pivot
+        for side in range(2):
+            done[side].append(head[side])
+        rest = tail
+    out = []
     for side in range(2):
-        whole = jnp.concatenate(out[side], axis=0)
+        whole = jnp.concatenate(done[side], axis=0)
         diag = lane == row + side * RANK
         pivots = jnp.sum(jnp.where(diag, whole, 0.0), axis=1, keepdims=True)
-        done.append(pltpu.roll(whole * lax.rsqrt(pivots), RANK, 1))
-    return jnp.where(low, done[0], 0.0), jnp.where(low, 0.0, done[1])
+        out.append(pltpu.roll(whole * lax.rsqrt(pivots), RANK, 1))
+    return jnp.where(low, out[0], 0.0), jnp.where(low, 0.0, out[1])
 
 
 def step_kernel(
@@ -140,6 +152,15 @@
 
     sent = []
 
+    def take():
+        old = sent[:]
+        sent.clear()
+        return old
+
+    def settle(copies):
+        for copy in copies:
+            copy.wait_send()
+
     far = [(2, 1), (1, 1), (3, 1), (2, 0), (1, 0), (3, 0), (0, 1)]
 
     def quarter(slot, q):
@@ -197,10 +218,12 @@
     for t in range(NZ):
         lbuf[t] = part[8 * t : 8 * t + 8]
     r1[r] = lbuf[z]
+    old = take()
     peers = [(1, d) for d in (4, 3, 5, 2, 6, 1, 7, 0)] + [(0, d) for d in (4, 3, 5, 2, 6, 1, 7)]
     for i, (over, dz) in enumerate(peers):
         dev = device(x, flip if over else y, at_z(dz), c)
         sent.append(send(lbuf.at[at_z(dz)], r1.at[r], b_ss.at[i], b_rs.at[i], dev))
+    settle(old)
     for i, (over, dz) in enumerate(peers):
         slot = ((1 - y_lo) if over else y_lo) * NZ + lax.rem(z + NZ - dz, NZ)
         arrival(r1.at[slot], b_ss.at[i], b_rs.at[i], mate)
@@ -209,8 +232,10 @@
         total = total + r1[t]
     lt2[z] = total / REPLICAS
     zs = (4, 3, 5, 2, 6, 1, 7)
+    old = take()
     for i, dz in enumerate(zs):
         sent.append(send(lt2.at[z], lt2.at[z], b2_ss.at[i], b2_rs.at[i], device(x, y, at_z(dz), c)))
+    settle(old)
     for i, dz in enumerate(zs):
         arrival(lt2.at[lax.rem(z + NZ - dz, NZ)], b2_ss.at[i], b2_rs.at[i], mate)
 
@@ -225,9 +250,11 @@
     sent.append(copy)
     chip = y_hi * NX + x
     c1[chip] = gp[c] + cpair[...]
+    old = take()
     for i, (dx, over) in enumerate(far):
         dev = device(at_x(dx), cross if over else y, z, c)
         sent.append(send(c1.at[chip], c1.at[chip], c1_ss.at[i], c1_rs.at[i], dev))
+    settle(old)
     for i, (dx, over) in enumerate(far):
         arrival(c1.at[lax.div(slots[i], NC)], c1_ss.at[i], c1_rs.at[i], mate)
     total = c1[0]
@@ -261,6 +288,7 @@
         return device(x, at_y(d), z, c) if pq == 0 else device(at_x(d), y, z, c)
 
     pair_copies = {}
+    old = take()
     for j, dj in enumerate(ds):
         for pq in range(2):
             i2 = second(pq, dj)
@@ -274,11 +302,11 @@
             pair_copies[pq, j] = send(
                 obuf.at[pq, i2], pr.at[pq, i2], e0_ss.at[pq, j], e0_rs.at[pq, j], mate
             )
+    settle(old)
     for j, dj in enumerate(ds):
         for pq in range(2):
             i2 = second(pq, dj)
             pair_copies[pq, j].wait_recv()
-            sent.append(pair_copies[pq, j])
             for k, dk in enumerate(ds):
                 i1 = first(pq, dk)
                 total = wbuf[pq, i2, i1] + pr[pq, i2, i1].astype(F32)
@@ -289,6 +317,7 @@
                     sent.append(
                         send(s1.at[pq, j, k], r2.at[pq, j, k], e1_ss.at[pq, j, k], e1_rs.at[pq, j, k], dev1(pq, dk))
                     )
+    settle(copy for copy in pair_copies.values())
     for j, dj in enumerate(ds):
         for pq in range(2):
             i1, i2 = first(pq, 0), second(pq, dj)
@@ -303,6 +332,7 @@
                 sent.append(
                     send(s2.at[pq, j], r3.at[pq, j], e2_ss.at[pq, j], e2_rs.at[pq, j], dev2(pq, dj))
                 )
+    settle(take())
     for pq in range(2):
         i1, i2 = first(pq, 0), second(pq, 0)
         total = wbuf[pq, i2, i1]
@@ -311,9 +341,12 @@
             total = total + r3[pq, j].astype(F32)
         wbuf[pq, i2, i1] = total
         s3[:, pq] = total.astype(BF16)
+    old = take()
     for i, dz in enumerate(zs):
         there = at_z(dz)
         sent.append(send(s3.at[there], r4.at[i], e3_ss.at[i], e3_rs.at[i], device(x, y, there, c)))
+    settle(old)
+    last = take()
     for i in range(7):
         arrival(r4.at[i], e3_ss.at[i], e3_rs.at[i], mate)
     for pq in range(2):
@@ -327,6 +360,8 @@
         piece = fbuf.at[c, pq, first(pq, 0), second(pq, 0), z]
         for i, dz in enumerate(zs):
             sent.append(send(piece, piece, g3_ss.at[pq, i], g3_rs.at[pq, i], device(x, y, at_z(dz), c)))
+    settle(last)
+    last = take()
     ortho = jnp.concatenate([obl[0], obl[1]], axis=0).T.astype(BF16)
 
     def sub_piece(pq, k, j):
@@ -347,11 +382,14 @@
         for k in range(3):
             sent.append(send(piece, piece, g2_ss.at[pq, k], g2_rs.at[pq, k], dev2(pq, ds[k])))
         spread(pq, 3)
+    settle(last)
     for j in (1, 2, 0):
         for pq in range(2):
             arrival(sub_piece(pq, 3, j), g2_ss.at[pq, j], g2_rs.at[pq, j], mate)
             spread(pq, j)
 
+    old = take()
+    settle(old[:6])
     stores = []
 
     def finish(n, pq, k):
@@ -371,21 +409,9 @@
             rest = (mbuf[pq * 16 + i1 * 4 + i].astype(F32) - approx).astype(BF16)
             approx = approx.astype(BF16)
             cols = pl.ds(pl.multiple_of(at + i * COL, COL), COL)
-            for m in range(2):
-                grads[m, :, cols] = approx[m * ROWS : m * ROWS + ROWS]
-                errors[m, :, cols] = rest[m * ROWS : m * ROWS + ROWS]
-        cols = pl.ds(at, 1024)
-        for i, (src, dst) in enumerate(
-            (
-                (grads.at[0, :, cols], uk.at[:, cols]),
-                (errors.at[0, :, cols], nk.at[0, :, cols]),
-                (grads.at[1, :, cols], uv.at[:, cols]),
-                (errors.at[1, :, cols], nv.at[0, :, cols]),
-            )
-        ):
-            copy = pltpu.make_async_copy(src, dst, out_sem.at[n, i])
-            copy.start()
-            stores.append(copy)
+            for m, (u, e) in enumerate(((uk, nk), (uv, nv))):
+                u[:, cols] = approx[m * ROWS : m * ROWS + ROWS]
+                e[0, :, cols] = rest[m * ROWS : m * ROWS + ROWS]
 
     pending = None
     for k in (3, 1, 2, 0):
@@ -395,6 +421,8 @@
                     arrival(sub_piece(pq, k, j), g1_ss.at[pq, j, k], g1_rs.at[pq, j, k], mate)
             piece = fbuf.at[c, pq, first(pq, 4 - ds[k])]
             sent.append(send(piece, piece, g0_ss.at[pq, k], g0_rs.at[pq, k], mate))
+            if k == 0 and pq == 1:
+                settle(old[6:])
             if pending is not None:
                 finish(*pending)
             pending = (2 * k + pq, pq, k)
@@ -405,15 +433,24 @@
                 jnp.concatenate([fbuf[m, s // 8, s % 8 // 2, s % 2 * 2 + i, 2 * a + b] for b in range(2)], axis=1)
                 for a in range(4)
             ]
-            fstage[m, :, i * COL : (i + 1) * COL] = jnp.concatenate(rows, axis=0).astype(F32)
-    for m, dst in enumerate((fk, fv)):
-        copy = pltpu.make_async_copy(fstage.at[m], dst, fac_sem.at[m])
-        copy.start()
-        stores.append(copy)
+            (fk, fv)[m][:, i * COL : (i + 1) * COL] = jnp.concatenate(rows, axis=0).astype(F32)
     for copy in stores:
         copy.wait()
     for copy in sent:
         copy.wait_send()
+
+
+def flush_kernel(uk, nk, fk, uv, nv, fv, uk_out, nk_out, fk_out, uv_out, nv_out, fv_out, sems):
+    pairs = [(fk, fk_out), (fv, fv_out)]
+    for q in range(4):
+        rows = pl.ds(16 * q, 16)
+        pairs += [(uk.at[rows], uk_out.at[rows]), (uv.at[rows], uv_out.at[rows])]
+        pairs += [(nk.at[0, rows], nk_out.at[0, rows]), (nv.at[0, rows], nv_out.at[0, rows])]
+    copies = [pltpu.make_async_copy(src, dst, sems.at[i]) for i, (src, dst) in enumerate(pairs)]
+    for copy in copies:
+        copy.start()
+    for copy in copies:
+        copy.wait()
 
 
 def per_device(grad_key, error_key, prev_key, grad_val, error_val, prev_val):
@@ -439,21 +476,29 @@
         for _ in range(2):
             scratch.append(dma if n is None else dma(n))
     hbm = pl.BlockSpec(memory_space=pl.ANY)
-    out = pl.BlockSpec(memory_space=pl.ANY)
-    update = jax.ShapeDtypeStruct((ROWS, 8192), BF16)
-    rest = jax.ShapeDtypeStruct((1, ROWS, 8192), BF16)
-    factor = jax.ShapeDtypeStruct((RANK, BLK), F32)
-    uk, nk, fk, uv, nv, fv = pl.pallas_call(
+    out = pl.BlockSpec(memory_space=pltpu.VMEM)
+    shapes = [((ROWS, 8192), BF16), ((1, ROWS, 8192), BF16), ((RANK, BLK), F32)] * 2
+    operands = (grad_key, error_key, prev_key.T, grad_val, error_val, prev_val.T)
+    held = pl.pallas_call(
         step_kernel,
         name="exchange",
-        out_shape=(update, rest, factor, update, rest, factor),
+        out_shape=tuple(pltpu.VMEM(*one) for one in shapes),
         in_specs=[hbm] * 6,
         out_specs=(out,) * 6,
         scratch_shapes=scratch,
         compiler_params=pltpu.CompilerParams(
-            collective_id=0, has_side_effects=True, vmem_limit_bytes=60 * 2**20
+            collective_id=0, has_side_effects=True, vmem_limit_bytes=32 * 2**20
         ),
-    )(grad_key, error_key, prev_key.T, grad_val, error_val, prev_val.T)
+    )(*(pltpu.with_memory_space_constraint(one, pltpu.HBM) for one in operands))
+    uk, nk, fk, uv, nv, fv = pl.pallas_call(
+        flush_kernel,
+        name="flush",
+        out_shape=tuple(jax.ShapeDtypeStruct(*one) for one in shapes),
+        in_specs=[pl.BlockSpec(memory_space=pltpu.VMEM)] * 6,
+        out_specs=(hbm,) * 6,
+        scratch_shapes=[dma((20,))],
+        compiler_params=pltpu.CompilerParams(vmem_limit_bytes=2**21),
+    )(*(pltpu.with_memory_space_constraint(one, pltpu.VMEM) for one in held))
     return uk, nk, fk.T, uv, nv, fv.T
 
 

time: 93.6 us -> 84 us (0.90)
  local copies, waits for them, and re-layouts: 7.31 us -> 0 us
  Pallas kernels: 85.5 us -> 83.3 us
    unnamed x16 -> x0, local copies, waits for them, and re-layouts: 7.31 us -> none
    pallas_call x1 -> x2, Pallas kernels: 85.5 us -> 83.3 us  [the longest x1 81 us: per_device(): pl.pallas_call(step_kernel, name='exchange', out_shape=tuple((pltpu.VMEM(...]
where the time goes in v3:
time: 84 us; the launch traced here: 83.9 us
  Pallas kernels  83.3 us (99%)
    pallas_call x1, Pallas kernels, per_device(): pl.pallas_call(step_kernel, name='exchange', out_shape=tuple((pltpu.VMEM(...  81 us
    pallas_call x1, Pallas kernels, per_device(): pl.pallas_call(flush_kernel, name='flush', out_shape=tuple((jax.ShapeDtyp...  2.26 us

profile of v3, /device:TPU:1, one launch (start us, length us, event | category | flops | bytes accessed | tf_op | source)
XLA Modules:
  0.0 83.9 jit_solution(2478298681345153815)
XLA Ops:
  0.6 81.0 %exchange.1 = (bf16[64,8192]{1,0:T(8,128)(2,1)S(1)}, bf16[1,64,8192]{2,1,0:T(8,128)(2,1)S(1)}, f32[64,512]{1,0:T(8,128)S(1)}, bf16[64,8192]{1,0:T(8,128)(2,1)S(1...) custom-call(bf16[1,64,8192]{2,1,0:T(8,128)(2,1)} %gk.1, bf16[1,64,8192]{2,1,0:T(8,128)(2,1)} %ek.1, ...), custom_call_target="tpu_custom_call" | custom-call | tf_op jit(solution)/shard_map/exchange/pallas_call | solution.py:482
  81.7 2.3 %flush.1 = (bf16[64,8192]{1,0:T(8,128)(2,1)}, bf16[1,64,8192]{2,1,0:T(8,128)(2,1)}, f32[64,512]{1,0:T(8,128)}, bf16[64,8192]{1,0:T(8,128)(2,1)}, bf16[1,64,8192]{2,1,0:T(8,128)(2,1)}, /*index=5*/f32[64,512]{1,0:T(8,128)}) custom-call(bf16[64,8192]{1,0:T(8,128)(2,1)S(1)} %get-tuple-element.18.uk, bf16[1,64,8192]{2,1,0:T(8,128)(2,1)S(1)} %get-tuple-element.19.nk, ...), custom_call_target="tpu_custom_call" | custom-call | tf_op jit(solution)/shard_map/flush/pallas_call | solution.py:493

commit v4 on v3

v4 whole, which is shorter than its diff:
```python
import functools

import jax
import jax.numpy as jnp
from jax import lax
from jax.experimental import pallas as pl
from jax.experimental.pallas import tpu as pltpu
from jax.sharding import PartitionSpec as P

MESH = pl.DeviceIdType.MESH
F32, BF16 = jnp.float32, jnp.bfloat16
NX, NY, NZ, NC = 4, 4, 8, 2
REPLICAS = 16
RANK = 64
ROWS = 64
BLK = 512
BLKS = 16
COL = 256
COLS = 32
RIDGE = 1e-6
LAG = 4
NT = (((1,), (1,)), ((), ()))
NN = (((1,), (0,)), ((), ()))


def device(x, y, z, c):
    return (lax.rem(y, 2) * NZ + z, (lax.div(y, 2) * NX + x) * NC + c)


def send(src, dst, ssem, rsem, dev):
    copy = pltpu.make_async_remote_copy(
        src_ref=src, dst_ref=dst, send_sem=ssem, recv_sem=rsem, device_id=dev, device_id_type=MESH
    )
    copy.start()
    return copy


def arrival(dst, ssem, rsem, dev):
    pltpu.make_async_remote_copy(
        src_ref=dst, dst_ref=dst, send_sem=ssem, recv_sem=rsem, device_id=dev, device_id_type=MESH
    ).wait_recv()


def solve_rows(gram, left):
    row = lax.broadcasted_iota(jnp.int32, (RANK, RANK), 0)
    lane = lax.broadcasted_iota(jnp.int32, (RANK, RANK), 1)
    diag = lane == row
    trace = jnp.sum(jnp.where(diag, gram, 0.0))
    rest = (gram + jnp.where(diag, RIDGE * (trace / RANK), 0.0), left)
    sub = lax.broadcasted_iota(jnp.int32, (8, 128), 0)
    done = ([], [])
    for t in range(8):
        count = RANK - 8 * t
        head = [one[:8] for one in rest]
        tail = [one[8:] if t < 7 else None for one in rest]
        cols = [jnp.broadcast_to(rest[0][:, 8 * t + k : 8 * t + k + 1], (count, 128)) for k in range(8)]
        hcol = [col[:8] for col in cols]
        tcol = [col[8:] if t < 7 else None for col in cols]
        for k in range(8):
            inv = 1.0 / hcol[k][k : k + 1, :]
            across = [hcol[j][k : k + 1, :] for j in range(8)]
            pivot = [one[k : k + 1, :] for one in head]
            if k < 7:
                m = jnp.where(sub > k, hcol[k] * inv, 0.0)
                for j in range(k + 1, 8):
                    hcol[j] = hcol[j] - m * across[j]
                head = [head[0] - m[:, :RANK] * pivot[0], head[1] - m * pivot[1]]
            if t < 7:
                m = tcol[k] * inv
                for j in range(k + 1, 8):
                    tcol[j] = tcol[j] - m * across[j]
                tail = [tail[0] - m[:, :RANK] * pivot[0], tail[1] - m * pivot[1]]
        for i in range(2):
            done[i].append(head[i])
        rest = tail
    pivots = jnp.sum(jnp.where(diag, jnp.concatenate(done[0], axis=0), 0.0), axis=1, keepdims=True)
    return jnp.concatenate(done[1], axis=0) * lax.rsqrt(pivots)


def step_kernel(
    gk, ek, pk, gv, ev, pv,
    uk, nk, fk, uv, nv, fv,
    grads, errors, mbuf, mchip, pstage, pbuf, acc, lbuf, r1, lt2, c1, obuf,
    wbuf, s1, r2, s2, r3, s3, r4, fbuf,
    load_sem, p_ss, p_rs, m_ss, m_rs, o_ss, o_rs,
    a_ss, a_rs, q_ss, q_rs, b_ss, b_rs, b2_ss, b2_rs, c1_ss, c1_rs,
    e1_ss, e1_rs, e2_ss, e2_rs, e3_ss, e3_rs,
    g3_ss, g3_rs, g2_ss, g2_rs, g1_ss, g1_rs, g0_ss, g0_rs,
):
    r = lax.axis_index("replica")
    s = lax.axis_index("shard")
    y_lo, z = lax.div(r, NZ), lax.rem(r, NZ)
    y_hi, x, c = lax.div(s, NX * NC), lax.rem(lax.div(s, NC), NX), lax.rem(s, NC)
    y = 2 * y_hi + y_lo
    oc = 1 - c
    cross = lax.rem(y + 3 + 2 * y_lo, NY)
    flip = 2 * y_hi + 1 - y_lo
    mate = device(x, y, z, oc)

    def at_x(d):
        return lax.rem(x + d, NX)

    def at_y(d):
        return lax.rem(y + d, NY)

    def at_z(d):
        return lax.rem(z + d, NZ)

    chip = y_hi * NX + x
    own_prev = [
        pltpu.make_async_copy(src.at[pl.ds(32 * h, 32)], pstage.at[m, h], load_sem.at[4 + 2 * m + h])
        for m, src in enumerate((pk, pv))
        for h in range(2)
    ]
    loads = [
        pltpu.make_async_copy(gk.at[0], grads.at[0], load_sem.at[0]),
        pltpu.make_async_copy(ek.at[0], errors.at[0], load_sem.at[1]),
        pltpu.make_async_copy(gv.at[0], grads.at[1], load_sem.at[2]),
        pltpu.make_async_copy(ev.at[0], errors.at[1], load_sem.at[3]),
    ]
    partners = [device(x, flip, at_z(d), c) for d in (4, 3, 5, 2, 6, 1, 7)]
    partners += [device(x, y, at_z(d), c) for d in (4, 3, 5, 2, 6, 1, 7)]
    partners += [device(at_x(d), cross, z, c) for d in (2, 1, 3)]
    partners += [device(at_x(d), y, z, c) for d in (2, 1, 3)]
    partners += [device(x, at_y(d), z, c) for d in (2, 1, 3)]
    partners += [mate]
    barrier = pltpu.get_barrier_semaphore()
    for dev in partners:
        pl.semaphore_signal(barrier, inc=1, device_id=dev, device_id_type=MESH)
    for copy in own_prev + loads:
        copy.start()
    for copy in own_prev:
        copy.wait()
    pl.semaphore_wait(barrier, len(partners))

    sent = []

    def take():
        old = sent[:]
        sent.clear()
        return old

    def settle(copies):
        for copy in copies:
            copy.wait_send()

    copy = send(pstage.at[oc], pbuf.at[chip, pl.ds(2 * c, 2)], p_ss, p_rs, mate)
    sent.append(copy)
    pbuf[chip, pl.ds(2 * c, 2)] = pstage[c]
    arrival(pbuf.at[chip, pl.ds(2 * oc, 2)], p_ss, p_rs, mate)
    far = [(2, 1), (1, 1), (3, 1), (2, 0), (1, 0), (3, 0), (0, 1)]

    def quarter(one, q):
        return pbuf.at[one, lax.rem(q, 4)]

    color = z + 2 * y_lo
    for i, (dx, over) in enumerate(far):
        dev = device(at_x(dx), cross if over else y, z, c)
        piece = quarter(chip, color + 2 * over)
        sent.append(send(piece, piece, a_ss.at[i], a_rs.at[i], dev))
    near = (device(x, flip, z, c), device(x, y, at_z(1), c), device(x, y, at_z(7), c))

    for copy in loads:
        copy.wait()

    def merge(b, carry):
        cols = pl.ds(pl.multiple_of(b * COL, COL), COL)
        for m in range(2):
            total = grads[m, :, cols].astype(F32) + errors[m, :, cols].astype(F32)
            mbuf[m, b] = total.astype(BF16)
        mchip[c, b] = mbuf[c, b]
        return carry

    lax.fori_loop(0, COLS, merge, 0)
    for t in range(4):
        part = pl.ds(8 * t, 8)
        sent.append(send(mbuf.at[oc, part], mchip.at[c, part], m_ss.at[t], m_rs.at[t], mate))

    def block_of(b):
        return jnp.concatenate([mchip[0, b], mchip[1, b]], axis=0)

    def left_term(one):
        total = None
        for bit in range(2):
            for h in range(2):
                cols = slice(h * COL, h * COL + COL)
                prev = jnp.concatenate([pbuf[one, 2 * bit, :, cols], pbuf[one, 2 * bit + 1, :, cols]], axis=0)
                term = lax.dot_general(prev, block_of(4 * one + 2 * bit + h), NT, preferred_element_type=F32)
                total = term if total is None else total + term
        return total

    order = (4, 5, 6, 1, 2, 3, 0)
    chips = []
    for i, (dx, over) in enumerate(far):
        yy = (1 - y_hi) if over else y_hi
        chips.append(yy * NX + lax.rem(x + NX - dx, NX))
    for i in order:
        piece = quarter(chips[i], color)
        arrival(piece, a_ss.at[i], a_rs.at[i], mate)
        for n in range(3):
            sent.append(send(piece, piece, q_ss.at[i, n], q_rs.at[i, n], near[n]))
    for t in range(4):
        arrival(mchip.at[oc, pl.ds(8 * t, 8)], m_ss.at[t], m_rs.at[t], mate)
    acc[...] = left_term(chip)
    for i in order:
        for n in range(3):
            arrival(quarter(chips[i], color + (2, 3, 1)[n]), q_ss.at[i, n], q_rs.at[i, n], mate)
        acc[...] += left_term(chips[i])

    for t in range(NZ):
        lbuf[t] = acc[8 * t : 8 * t + 8, :]
    r1[r] = lbuf[z]
    old = take()
    peers = [(1, d) for d in (4, 3, 5, 2, 6, 1, 7, 0)] + [(0, d) for d in (4, 3, 5, 2, 6, 1, 7)]
    for i, (over, dz) in enumerate(peers):
        dev = device(x, flip if over else y, at_z(dz), c)
        sent.append(send(lbuf.at[at_z(dz)], r1.at[r], b_ss.at[i], b_rs.at[i], dev))
    settle(old)
    for i, (over, dz) in enumerate(peers):
        slot = ((1 - y_lo) if over else y_lo) * NZ + lax.rem(z + NZ - dz, NZ)
        arrival(r1.at[slot], b_ss.at[i], b_rs.at[i], mate)
    total = r1[0]
    for t in range(1, REPLICAS):
        total = total + r1[t]
    lt2[z] = total / REPLICAS
    zs = (4, 3, 5, 2, 6, 1, 7)
    old = take()
    for i, dz in enumerate(zs):
        sent.append(send(lt2.at[z], lt2.at[z], b2_ss.at[i], b2_rs.at[i], device(x, y, at_z(dz), c)))
    settle(old)
    for i, dz in enumerate(zs):
        arrival(lt2.at[lax.rem(z + NZ - dz, NZ)], b2_ss.at[i], b2_rs.at[i], mate)

    left = jnp.concatenate([lt2[t] for t in range(NZ)], axis=0)
    gram = lax.dot_general(left, left, NT, precision=lax.Precision.HIGHEST, preferred_element_type=F32)
    c1[chip] = jnp.concatenate([gram[0:32], gram[32:64]], axis=1)
    old = take()
    for i, (dx, over) in enumerate(far):
        dev = device(at_x(dx), cross if over else y, z, c)
        sent.append(send(c1.at[chip], c1.at[chip], c1_ss.at[i], c1_rs.at[i], dev))
    settle(old)
    for i in range(7):
        arrival(c1.at[chips[i]], c1_ss.at[i], c1_rs.at[i], mate)
    total = c1[0]
    for t in range(1, 8):
        total = total + c1[t]
    gram = jnp.concatenate([total[:, :RANK], total[:, RANK:]], axis=0)

    ortho = solve_rows(gram, left).astype(BF16)
    obuf[c] = ortho
    old = take()
    copy = send(obuf.at[c], obuf.at[c], o_ss, o_rs, mate)
    sent.append(copy)

    firsts = (x, y)
    seconds = (y, x)
    ds = (2, 1, 3, 0)

    def first(pq, d):
        return lax.rem(firsts[pq] + d, 4)

    def second(pq, d):
        return lax.rem(seconds[pq] + d, 4)

    def dev1(pq, d):
        return device(at_x(d), y, z, c) if pq == 0 else device(x, at_y(d), z, c)

    def dev2(pq, d):
        return device(x, at_y(d), z, c) if pq == 0 else device(at_x(d), y, z, c)

    for j, dj in enumerate(ds):
        for pq in range(2):
            i2 = second(pq, dj)
            for k, dk in enumerate(ds):
                block = block_of(pq * 16 + first(pq, dk) * 4 + i2)
                term = lax.dot_general(ortho, block, NN, preferred_element_type=F32)
                for a in range(4):
                    for b in range(2):
                        tile = term[16 * a : 16 * a + 16, b * 128 : b * 128 + 128]
                        if dk == 0:
                            wbuf[pq, j, 2 * a + b] = tile
                        else:
                            s1[pq, j, k, 2 * a + b] = tile.astype(BF16)
                if dk != 0:
                    sent.append(
                        send(s1.at[pq, j, k], r2.at[pq, j, k], e1_ss.at[pq, j, k], e1_rs.at[pq, j, k], dev1(pq, dk))
                    )
    settle(old)
    for j, dj in enumerate(ds):
        for pq in range(2):
            total = wbuf[pq, j]
            for k in range(3):
                arrival(r2.at[pq, j, k], e1_ss.at[pq, j, k], e1_rs.at[pq, j, k], mate)
                total = total + r2[pq, j, k].astype(F32)
            if dj == 0:
                wbuf[pq, j] = total
            else:
                s2[pq, j] = total.astype(BF16)
                sent.append(
                    send(s2.at[pq, j], r3.at[pq, j], e2_ss.at[pq, j], e2_rs.at[pq, j], dev2(pq, dj))
                )
    settle(take())
    for pq in range(2):
        total = wbuf[pq, 3]
        for j in range(3):
            arrival(r3.at[pq, j], e2_ss.at[pq, j], e2_rs.at[pq, j], mate)
            total = total + r3[pq, j].astype(F32)
        wbuf[pq, 3] = total
        s3[:, pq] = total.astype(BF16)
    old = take()
    for i, dz in enumerate(zs):
        there = at_z(dz)
        sent.append(send(s3.at[there], r4.at[i], e3_ss.at[i], e3_rs.at[i], device(x, y, there, c)))
    settle(old)
    last = take()
    for i in range(7):
        arrival(r4.at[i], e3_ss.at[i], e3_rs.at[i], mate)
    for pq in range(2):
        i1, i2 = first(pq, 0), second(pq, 0)
        total = wbuf[pq, 3, z]
        for i in range(7):
            total = total + r4[i, pq].astype(F32)
        fbuf[c, pq, i1, i2, z] = (total / REPLICAS).astype(BF16)

    for pq in range(2):
        piece = fbuf.at[c, pq, first(pq, 0), second(pq, 0), z]
        for i, dz in enumerate(zs):
            sent.append(send(piece, piece, g3_ss.at[pq, i], g3_rs.at[pq, i], device(x, y, at_z(dz), c)))
    settle(last)
    last = take()
    arrival(obuf.at[oc], o_ss, o_rs, mate)
    wide = []
    for m in range(2):
        turned = obuf[m].astype(F32).T
        turned = jnp.where(c == 0, turned[:ROWS], turned[ROWS:])
        none = jnp.zeros((ROWS, RANK), F32)
        wide.append(jnp.concatenate([turned, none] if m == 0 else [none, turned], axis=1))
    wide = jnp.concatenate(wide, axis=0).astype(BF16)

    def sub_piece(pq, k, j):
        return fbuf.at[c, pq, first(pq, 4 - ds[k]), second(pq, 4 - ds[j])]

    def pass_on(pq, k, j):
        piece = sub_piece(pq, k, j)
        sent.append(send(piece, piece, g0_ss.at[pq, k, j], g0_rs.at[pq, k, j], mate))
        chunks.append((pq, k, j))

    def spread(pq, j):
        piece = sub_piece(pq, 3, j)
        for k in range(3):
            sent.append(send(piece, piece, g1_ss.at[pq, j, k], g1_rs.at[pq, j, k], dev1(pq, ds[k])))
        pass_on(pq, 3, j)

    def finish(pq, k, j):
        i1, i2 = first(pq, 4 - ds[k]), second(pq, 4 - ds[j])
        arrival(fbuf.at[oc, pq, i1, i2], g0_ss.at[pq, k, j], g0_rs.at[pq, k, j], mate)
        sides = []
        for m in range(2):
            tiles = fbuf[m, pq, i1, i2]
            rows = [jnp.concatenate([tiles[2 * a], tiles[2 * a + 1]], axis=1) for a in range(4)]
            sides.append(jnp.concatenate(rows, axis=0))
        factor = jnp.concatenate(sides, axis=0)
        approx = lax.dot_general(wide, factor, NN, preferred_element_type=F32)
        block = pq * 16 + i1 * 4 + i2
        merged = jnp.concatenate([mbuf[0, block], mbuf[1, block]], axis=0)
        rest = (merged.astype(F32) - approx).astype(BF16)
        approx = approx.astype(BF16)
        cols = pl.ds(pl.multiple_of(block * COL, COL), COL)
        for m, (u, e) in enumerate(((uk, nk), (uv, nv))):
            u[:, cols] = approx[m * ROWS : m * ROWS + ROWS]
            e[0, :, cols] = rest[m * ROWS : m * ROWS + ROWS]

    chunks = []
    for pq in range(2):
        piece = sub_piece(pq, 3, 3)
        for i, dz in enumerate(zs):
            arrival(
                fbuf.at[c, pq, first(pq, 0), second(pq, 0), lax.rem(z + NZ - dz, NZ)],
                g3_ss.at[pq, i], g3_rs.at[pq, i], mate,
            )
        for k in range(3):
            sent.append(send(piece, piece, g2_ss.at[pq, k], g2_rs.at[pq, k], dev2(pq, ds[k])))
        spread(pq, 3)
    settle(last)
    for j in (1, 2, 0):
        for pq in range(2):
            arrival(sub_piece(pq, 3, j), g2_ss.at[pq, j], g2_rs.at[pq, j], mate)
            spread(pq, j)
    for j in (3, 1, 2, 0):
        for pq in range(2):
            for k in (1, 2, 0):
                arrival(sub_piece(pq, k, j), g1_ss.at[pq, j, k], g1_rs.at[pq, j, k], mate)
                pass_on(pq, k, j)
                if len(chunks) > LAG:
                    finish(*chunks.pop(0))
    while chunks:
        finish(*chunks.pop(0))
    for i in range(2):
        for m in range(2):
            rows = [
                jnp.concatenate([fbuf[m, s // 8, s % 8 // 2, s % 2 * 2 + i, 2 * a + b] for b in range(2)], axis=1)
                for a in range(4)
            ]
            (fk, fv)[m][:, i * COL : (i + 1) * COL] = jnp.concatenate(rows, axis=0).astype(F32)
    for copy in sent:
        copy.wait_send()


def flush_kernel(uk, nk, fk, uv, nv, fv, uk_out, nk_out, fk_out, uv_out, nv_out, fv_out, sems):
    pairs = [(fk, fk_out), (fv, fv_out)]
    for q in range(4):
        rows = pl.ds(16 * q, 16)
        pairs += [(uk.at[rows], uk_out.at[rows]), (uv.at[rows], uv_out.at[rows])]
        pairs += [(nk.at[0, rows], nk_out.at[0, rows]), (nv.at[0, rows], nv_out.at[0, rows])]
    copies = [pltpu.make_async_copy(src, dst, sems.at[i]) for i, (src, dst) in enumerate(pairs)]
    for copy in copies:
        copy.start()
    for copy in copies:
        copy.wait()


def per_device(grad_key, error_key, prev_key, grad_val, error_val, prev_val):
    vm = pltpu.VMEM
    dma = pltpu.SemaphoreType.DMA
    scratch = [
        vm((2, ROWS, 8192), BF16), vm((2, ROWS, 8192), BF16),
        vm((2, COLS, ROWS, COL), BF16), vm((2, COLS, ROWS, COL), BF16),
        vm((2, 2, 32, BLK), BF16), vm((8, 4, 32, BLK), BF16),
        vm((RANK, 128), F32), vm((8, 8, 128), F32), vm((16, 8, 128), F32), vm((8, 8, 128), F32),
        vm((8, 32, 128), F32), vm((2, RANK, 128), BF16),
        vm((2, 4, 8, 16, 128), F32),
        vm((2, 4, 3, 8, 16, 128), BF16), vm((2, 4, 3, 8, 16, 128), BF16),
        vm((2, 3, 8, 16, 128), BF16), vm((2, 3, 8, 16, 128), BF16),
        vm((8, 2, 16, 128), BF16), vm((7, 2, 16, 128), BF16),
        vm((2, 2, 4, 4, 8, 16, 128), BF16),
        dma((8,)),
    ]
    for n in (
        None, (4,), None, (7,), (7, 3), (15,), (7,), (7,),
        (2, 4, 3), (2, 3), (7,), (2, 7), (2, 3), (2, 4, 3), (2, 4, 4),
    ):
        for _ in range(2):
            scratch.append(dma if n is None else dma(n))
    hbm = pl.BlockSpec(memory_space=pl.ANY)
    out = pl.BlockSpec(memory_space=pltpu.VMEM)
    shapes = [((ROWS, 8192), BF16), ((1, ROWS, 8192), BF16), ((RANK, BLK), F32)] * 2
    operands = (grad_key, error_key, prev_key.T, grad_val, error_val, prev_val.T)
    held = pl.pallas_call(
        step_kernel,
        name="exchange",
        out_shape=tuple(pltpu.VMEM(*one) for one in shapes),
        in_specs=[hbm] * 6,
        out_specs=(out,) * 6,
        scratch_shapes=scratch,
        compiler_params=pltpu.CompilerParams(
            collective_id=0, has_side_effects=True, vmem_limit_bytes=32 * 2**20
        ),
    )(*(pltpu.with_memory_space_constraint(one, pltpu.HBM) for one in operands))
    uk, nk, fk, uv, nv, fv = pl.pallas_call(
        flush_kernel,
        name="flush",
        out_shape=tuple(jax.ShapeDtypeStruct(*one) for one in shapes),
        in_specs=[pl.BlockSpec(memory_space=pltpu.VMEM)] * 6,
        out_specs=(hbm,) * 6,
        scratch_shapes=[dma((20,))],
        compiler_params=pltpu.CompilerParams(vmem_limit_bytes=2**21),
    )(*(pltpu.with_memory_space_constraint(one, pltpu.VMEM) for one in held))
    return uk, nk, fk.T, uv, nv, fv.T


def solution(mesh):
    wide = P("replica", "shard", None)
    flat = P("shard", None)
    return jax.shard_map(
        per_device,
        mesh=mesh,
        in_specs=(wide, wide, flat, wide, wide, flat),
        out_specs=(flat, wide, flat, flat, wide, flat),
        check_vma=False,
    )
```

time: 84 us -> 78.2 us (0.931)
  Pallas kernels: 83.3 us -> 77.5 us
    pallas_call x1, Pallas kernels: 81 us -> 75.2 us  [per_device(): pl.pallas_call(step_kernel, name='exchange', out_shape=tuple((pltpu.VMEM(...]
where the time goes in v4:
time: 78.2 us; the launch traced here: 78.1 us
  Pallas kernels  77.5 us (99%)
    pallas_call x1, Pallas kernels, per_device(): pl.pallas_call(step_kernel, name='exchange', out_shape=tuple((pltpu.VMEM(...  75.2 us
    pallas_call x1, Pallas kernels, per_device(): pl.pallas_call(flush_kernel, name='flush', out_shape=tuple((jax.ShapeDtyp...  2.26 us

profile of v4, /device:TPU:1, one launch (start us, length us, event | category | flops | bytes accessed | tf_op | source)
XLA Modules:
  0.0 78.1 jit_solution(15174465634963403333)
XLA Ops:
  0.6 75.2 %exchange.1 = (bf16[64,8192]{1,0:T(8,128)(2,1)S(1)}, bf16[1,64,8192]{2,1,0:T(8,128)(2,1)S(1)}, f32[64,512]{1,0:T(8,128)S(1)}, bf16[64,8192]{1,0:T(8,128)(2,1)S(1...) custom-call(bf16[1,64,8192]{2,1,0:T(8,128)(2,1)} %gk.1, bf16[1,64,8192]{2,1,0:T(8,128)(2,1)} %ek.1, ...), custom_call_target="tpu_custom_call" | custom-call | tf_op jit(solution)/shard_map/exchange/pallas_call | solution.py:448
  75.8 2.3 %flush.1 = (bf16[64,8192]{1,0:T(8,128)(2,1)}, bf16[1,64,8192]{2,1,0:T(8,128)(2,1)}, f32[64,512]{1,0:T(8,128)}, bf16[64,8192]{1,0:T(8,128)(2,1)}, bf16[1,64,8192]{2,1,0:T(8,128)(2,1)}, /*index=5*/f32[64,512]{1,0:T(8,128)}) custom-call(bf16[64,8192]{1,0:T(8,128)(2,1)S(1)} %get-tuple-element.18.uk, bf16[1,64,8192]{2,1,0:T(8,128)(2,1)S(1)} %get-tuple-element.19.nk, ...), custom_call_target="tpu_custom_call" | custom-call | tf_op jit(solution)/shard_map/flush/pallas_call | solution.py:459

commit v5 on v4

--- a/solution.py
+++ b/solution.py
@@ -123,6 +123,8 @@
     partners += [device(at_x(d), cross, z, c) for d in (2, 1, 3)]
     partners += [device(at_x(d), y, z, c) for d in (2, 1, 3)]
     partners += [device(x, at_y(d), z, c) for d in (2, 1, 3)]
+    partners += [device(at_x(d), cross, z, oc) for d in (2, 1, 3, 0)]
+    partners += [device(at_x(d), y, z, oc) for d in (2, 1, 3)]
     partners += [mate]
     barrier = pltpu.get_barrier_semaphore()
     for dev in partners:
@@ -144,20 +146,30 @@
         for copy in copies:
             copy.wait_send()
 
+    far = [(2, 1), (1, 1), (3, 1), (2, 0), (1, 0), (3, 0), (0, 1)]
+
+    def quarter(one, q):
+        return pbuf.at[one, lax.rem(q, 4)]
+
+    color = z + 2 * y_lo
+    along = c == lax.rem(lax.div(color, 2), 2)
+    half = lax.rem(color, 2)
+    row = jnp.where(along, y, cross)
+    there = quarter(chip, color + jnp.where(along, 0, 2))
+    place = jnp.where(along, 3, 0)
+    for i in range(3):
+        for m in range(2):
+            dev = device(at_x(far[i][0]), row, z, m)
+            sent.append(send(pstage.at[m, half], there, a_ss.at[m, i], a_rs.at[place + i], dev))
+
+    @pl.when(jnp.logical_not(along))
+    def _():
+        for m in range(2):
+            send(pstage.at[m, half], there, a_ss.at[m, 3], a_rs.at[6], device(x, cross, z, m))
+
     copy = send(pstage.at[oc], pbuf.at[chip, pl.ds(2 * c, 2)], p_ss, p_rs, mate)
     sent.append(copy)
     pbuf[chip, pl.ds(2 * c, 2)] = pstage[c]
-    arrival(pbuf.at[chip, pl.ds(2 * oc, 2)], p_ss, p_rs, mate)
-    far = [(2, 1), (1, 1), (3, 1), (2, 0), (1, 0), (3, 0), (0, 1)]
-
-    def quarter(one, q):
-        return pbuf.at[one, lax.rem(q, 4)]
-
-    color = z + 2 * y_lo
-    for i, (dx, over) in enumerate(far):
-        dev = device(at_x(dx), cross if over else y, z, c)
-        piece = quarter(chip, color + 2 * over)
-        sent.append(send(piece, piece, a_ss.at[i], a_rs.at[i], dev))
     near = (device(x, flip, z, c), device(x, y, at_z(1), c), device(x, y, at_z(7), c))
 
     for copy in loads:
@@ -201,11 +213,20 @@
             sent.append(send(piece, piece, q_ss.at[i, n], q_rs.at[i, n], near[n]))
     for t in range(4):
         arrival(mchip.at[oc, pl.ds(8 * t, 8)], m_ss.at[t], m_rs.at[t], mate)
+    arrival(pbuf.at[chip, pl.ds(2 * oc, 2)], p_ss, p_rs, mate)
     acc[...] = left_term(chip)
     for i in order:
         for n in range(3):
             arrival(quarter(chips[i], color + (2, 3, 1)[n]), q_ss.at[i, n], q_rs.at[i, n], mate)
         acc[...] += left_term(chips[i])
+
+    @pl.when(jnp.logical_not(along))
+    def _():
+        for m in range(2):
+            pltpu.make_async_remote_copy(
+                src_ref=pstage.at[m, half], dst_ref=there, send_sem=a_ss.at[m, 3], recv_sem=a_rs.at[6],
+                device_id=mate, device_id_type=MESH,
+            ).wait_send()
 
     for t in range(NZ):
         lbuf[t] = acc[8 * t : 8 * t + 8, :]
@@ -370,6 +391,10 @@
             u[:, cols] = approx[m * ROWS : m * ROWS + ROWS]
             e[0, :, cols] = rest[m * ROWS : m * ROWS + ROWS]
 
+    def settle_some():
+        for _ in range(min(3, len(sent) - 6)):
+            sent.pop(0).wait_send()
+
     chunks = []
     for pq in range(2):
         piece = sub_piece(pq, 3, 3)
@@ -391,9 +416,11 @@
             for k in (1, 2, 0):
                 arrival(sub_piece(pq, k, j), g1_ss.at[pq, j, k], g1_rs.at[pq, j, k], mate)
                 pass_on(pq, k, j)
+                settle_some()
                 if len(chunks) > LAG:
                     finish(*chunks.pop(0))
     while chunks:
+        settle_some()
         finish(*chunks.pop(0))
     for i in range(2):
         for m in range(2):
@@ -436,11 +463,11 @@
         dma((8,)),
     ]
     for n in (
-        None, (4,), None, (7,), (7, 3), (15,), (7,), (7,),
-        (2, 4, 3), (2, 3), (7,), (2, 7), (2, 3), (2, 4, 3), (2, 4, 4),
+        None, None, (4,), (4,), None, None, (2, 4), (7,), (7, 3), (7, 3), (15,), (15,), (7,), (7,), (7,), (7,),
+        (2, 4, 3), (2, 4, 3), (2, 3), (2, 3), (7,), (7,),
+        (2, 7), (2, 7), (2, 3), (2, 3), (2, 4, 3), (2, 4, 3), (2, 4, 4), (2, 4, 4),
     ):
-        for _ in range(2):
-            scratch.append(dma if n is None else dma(n))
+        scratch.append(dma if n is None else dma(n))
     hbm = pl.BlockSpec(memory_space=pl.ANY)
     out = pl.BlockSpec(memory_space=pltpu.VMEM)
     shapes = [((ROWS, 8192), BF16), ((1, ROWS, 8192), BF16), ((RANK, BLK), F32)] * 2

time: 78.2 us -> 77.2 us (0.987)
  Pallas kernels: 77.5 us -> 76.4 us
    pallas_call x1, Pallas kernels: 75.2 us -> 74.2 us  [per_device(): pl.pallas_call(step_kernel, name='exchange', out_shape=tuple((pltpu.VMEM(...]
where the time goes in v5:
time: 77.2 us; the launch traced here: 77.1 us
  Pallas kernels  76.4 us (99%)
    pallas_call x1, Pallas kernels, per_device(): pl.pallas_call(step_kernel, name='exchange', out_shape=tuple((pltpu.VMEM(...  74.2 us
    pallas_call x1, Pallas kernels, per_device(): pl.pallas_call(flush_kernel, name='flush', out_shape=tuple((jax.ShapeDtyp...  2.26 us

profile of v5, /device:TPU:1, one launch (start us, length us, event | category | flops | bytes accessed | tf_op | source)
XLA Modules:
  0.0 77.1 jit_solution(5692322939059385682)
XLA Ops:
  0.6 74.2 %exchange.1 = (bf16[64,8192]{1,0:T(8,128)(2,1)S(1)}, bf16[1,64,8192]{2,1,0:T(8,128)(2,1)S(1)}, f32[64,512]{1,0:T(8,128)S(1)}, bf16[64,8192]{1,0:T(8,128)(2,1)S(1...) custom-call(bf16[1,64,8192]{2,1,0:T(8,128)(2,1)} %gk.1, bf16[1,64,8192]{2,1,0:T(8,128)(2,1)} %ek.1, ...), custom_call_target="tpu_custom_call" | custom-call | tf_op jit(solution)/shard_map/exchange/pallas_call | solution.py:475
  74.8 2.3 %flush.1 = (bf16[64,8192]{1,0:T(8,128)(2,1)}, bf16[1,64,8192]{2,1,0:T(8,128)(2,1)}, f32[64,512]{1,0:T(8,128)}, bf16[64,8192]{1,0:T(8,128)(2,1)}, bf16[1,64,8192]{2,1,0:T(8,128)(2,1)}, /*index=5*/f32[64,512]{1,0:T(8,128)}) custom-call(bf16[64,8192]{1,0:T(8,128)(2,1)S(1)} %get-tuple-element.18.uk, bf16[1,64,8192]{2,1,0:T(8,128)(2,1)S(1)} %get-tuple-element.19.nk, ...), custom_call_target="tpu_custom_call" | custom-call | tf_op jit(solution)/shard_map/flush/pallas_call | solution.py:486

commit v6 on v5

--- a/solution.py
+++ b/solution.py
@@ -57,7 +57,7 @@
         hcol = [col[:8] for col in cols]
         tcol = [col[8:] if t < 7 else None for col in cols]
         for k in range(8):
-            inv = 1.0 / hcol[k][k : k + 1, :]
+            inv = pl.reciprocal(hcol[k][k : k + 1, :])
             across = [hcol[j][k : k + 1, :] for j in range(8)]
             pivot = [one[k : k + 1, :] for one in head]
             if k < 7:
@@ -82,7 +82,7 @@
     uk, nk, fk, uv, nv, fv,
     grads, errors, mbuf, mchip, pstage, pbuf, acc, lbuf, r1, lt2, c1, obuf,
     wbuf, s1, r2, s2, r3, s3, r4, fbuf,
-    load_sem, p_ss, p_rs, m_ss, m_rs, o_ss, o_rs,
+    load_sem, token, p_ss, p_rs, m_ss, m_rs, o_ss, o_rs,
     a_ss, a_rs, q_ss, q_rs, b_ss, b_rs, b2_ss, b2_rs, c1_ss, c1_rs,
     e1_ss, e1_rs, e2_ss, e2_rs, e3_ss, e3_rs,
     g3_ss, g3_rs, g2_ss, g2_rs, g1_ss, g1_rs, g0_ss, g0_rs,
@@ -118,8 +118,8 @@
         pltpu.make_async_copy(gv.at[0], grads.at[1], load_sem.at[2]),
         pltpu.make_async_copy(ev.at[0], errors.at[1], load_sem.at[3]),
     ]
-    partners = [device(x, flip, at_z(d), c) for d in (4, 3, 5, 2, 6, 1, 7)]
-    partners += [device(x, y, at_z(d), c) for d in (4, 3, 5, 2, 6, 1, 7)]
+    close = (1, 7, 2, 6)
+    partners = [device(x, y, at_z(d), c) for d in (2, 6, 1, 7)]
     partners += [device(at_x(d), cross, z, c) for d in (2, 1, 3)]
     partners += [device(at_x(d), y, z, c) for d in (2, 1, 3)]
     partners += [device(x, at_y(d), z, c) for d in (2, 1, 3)]
@@ -137,6 +137,16 @@
 
     sent = []
 
+    def greet(turn):
+        for i, d in enumerate(close):
+            pl.semaphore_signal(
+                token.at[turn, i], inc=1, device_id=device(x, y, at_z(d), c), device_id_type=MESH
+            )
+
+    def greeted(turn):
+        for i in range(4):
+            pl.semaphore_wait(token.at[turn, i], 1)
+
     def take():
         old = sent[:]
         sent.clear()
@@ -172,6 +182,7 @@
     pbuf[chip, pl.ds(2 * c, 2)] = pstage[c]
     near = (device(x, flip, z, c), device(x, y, at_z(1), c), device(x, y, at_z(7), c))
 
+    greet(0)
     for copy in loads:
         copy.wait()
 
@@ -187,6 +198,9 @@
     for t in range(4):
         part = pl.ds(8 * t, 8)
         sent.append(send(mbuf.at[oc, part], mchip.at[c, part], m_ss.at[t], m_rs.at[t], mate))
+
+    greeted(0)
+    greet(1)
 
     def block_of(b):
         return jnp.concatenate([mchip[0, b], mchip[1, b]], axis=0)
@@ -231,6 +245,7 @@
     for t in range(NZ):
         lbuf[t] = acc[8 * t : 8 * t + 8, :]
     r1[r] = lbuf[z]
+    greeted(1)
     old = take()
     peers = [(1, d) for d in (4, 3, 5, 2, 6, 1, 7, 0)] + [(0, d) for d in (4, 3, 5, 2, 6, 1, 7)]
     for i, (over, dz) in enumerate(peers):
@@ -460,7 +475,7 @@
         vm((2, 3, 8, 16, 128), BF16), vm((2, 3, 8, 16, 128), BF16),
         vm((8, 2, 16, 128), BF16), vm((7, 2, 16, 128), BF16),
         vm((2, 2, 4, 4, 8, 16, 128), BF16),
-        dma((8,)),
+        dma((8,)), pltpu.SemaphoreType.REGULAR((2, 4)),
     ]
     for n in (
         None, None, (4,), (4,), None, None, (2, 4), (7,), (7, 3), (7, 3), (15,), (15,), (7,), (7,), (7,), (7,),

time: 77.2 us -> 77.2 us (level)
  no operation moved by 1% of the time
where the time goes in v6:
time: 77.2 us; the launch traced here: 77.1 us
  Pallas kernels  76.4 us (99%)
    pallas_call x1, Pallas kernels, per_device(): pl.pallas_call(step_kernel, name='exchange', out_shape=tuple((pltpu.VMEM(...  74.2 us
    pallas_call x1, Pallas kernels, per_device(): pl.pallas_call(flush_kernel, name='flush', out_shape=tuple((jax.ShapeDtyp...  2.26 us

profile of v6, /device:TPU:1, one launch (start us, length us, event | category | flops | bytes accessed | tf_op | source)
XLA Modules:
  0.0 77.1 jit_solution(7647608855824717477)
XLA Ops:
  0.6 74.2 %exchange.1 = (bf16[64,8192]{1,0:T(8,128)(2,1)S(1)}, bf16[1,64,8192]{2,1,0:T(8,128)(2,1)S(1)}, f32[64,512]{1,0:T(8,128)S(1)}, bf16[64,8192]{1,0:T(8,128)(2,1)S(1...) custom-call(bf16[1,64,8192]{2,1,0:T(8,128)(2,1)} %gk.1, bf16[1,64,8192]{2,1,0:T(8,128)(2,1)} %ek.1, ...), custom_call_target="tpu_custom_call" | custom-call | tf_op jit(solution)/shard_map/exchange/pallas_call | solution.py:490
  74.8 2.3 %flush.1 = (bf16[64,8192]{1,0:T(8,128)(2,1)}, bf16[1,64,8192]{2,1,0:T(8,128)(2,1)}, f32[64,512]{1,0:T(8,128)}, bf16[64,8192]{1,0:T(8,128)(2,1)}, bf16[1,64,8192]{2,1,0:T(8,128)(2,1)}, /*index=5*/f32[64,512]{1,0:T(8,128)}) custom-call(bf16[64,8192]{1,0:T(8,128)(2,1)S(1)} %get-tuple-element.18.uk, bf16[1,64,8192]{2,1,0:T(8,128)(2,1)S(1)} %get-tuple-element.19.nk, ...), custom_call_target="tpu_custom_call" | custom-call | tf_op jit(solution)/shard_map/flush/pallas_call | solution.py:501
